TPU v7x, 256 devices: a whole 4x4x8 slice. The times are simulated.
256 devices in a mesh: dp: 16 (over z, core), expert: 16 (over x, y).
Axes of the slice: x: 4, y: 4, z: 8, core: 2. Of those that a mesh axis runs over, the one named last changes fastest.
Arguments:
- tokens: bfloat16 [32768, 2048], P(('dp', 'expert')), may hold values from -6 to 6
- expert_ids: int32 [32768, 8], P(('dp', 'expert')), may hold values from 0 to 127, as said below
- gate_probs: float32 [32768, 8], P(('dp', 'expert')), may hold values from 0.1 to 1
- cotangent: bfloat16 [32768, 2048], P(('dp', 'expert')), may hold values from -1.5 to 1.5
- expert_weights: bfloat16 [2048, 16, 3, 768], P(None, 'expert'), may hold values from -0.21875 to 0.21875
Outputs:
- mixed: bfloat16 [32768, 2048], P(('dp', 'expert'))
- grad_tokens: bfloat16 [32768, 2048], P(('dp', 'expert'))
- grad_gates: float32 [32768, 8], P(('dp', 'expert'))
- grad_weights: bfloat16 [2048, 16, 3, 768], P('dp', 'expert')
Inputs may be any that keep to these rules, and one draw needn't show every extreme that they name: `expert_ids`: each row names 8 different experts. In the rows of one device every expert below 16 is named by 1 to 24 rows, and for every index of dp some such expert is named by exactly 24 rows of each device of that index.
All inputs are finite; a program needn't handle non-finite values.
Results may differ from a plain program's by a relative error of at most 0.0058.
Values may be sent and summed in bfloat16 or wider, within the bound.
A program may use at most 128 MiB of HBM per device.

v0:
```python
import jax
import jax.numpy as jnp
from jax import lax
from jax.sharding import PartitionSpec as P

BLOCK = 128
CAP = 24


def expert_rows(x_rows, dy_rows, weights):
    w_gate = weights[:, 0, :]
    w_up = weights[:, 1, :]
    w_down = weights[:, 2, :]
    contract_last = (((1,), (1,)), ((), ()))
    gate_proj = jnp.dot(x_rows, w_gate, preferred_element_type=jnp.float32)
    up_proj = jnp.dot(x_rows, w_up, preferred_element_type=jnp.float32)
    sigmoid_gate = jax.nn.sigmoid(gate_proj)
    silu_gate = gate_proj * sigmoid_gate
    hidden = (silu_gate * up_proj).astype(jnp.bfloat16)
    expert_out = lax.dot_general(
        hidden, w_down, contract_last, preferred_element_type=jnp.float32
    ).astype(jnp.bfloat16)
    hidden_grad = jnp.dot(dy_rows, w_down, preferred_element_type=jnp.float32)
    gate_grad = (
        hidden_grad * up_proj * sigmoid_gate * (1.0 + gate_proj * (1.0 - sigmoid_gate))
    ).astype(jnp.bfloat16)
    up_grad = (hidden_grad * silu_gate).astype(jnp.bfloat16)
    token_part = (
        lax.dot_general(gate_grad, w_gate, contract_last, preferred_element_type=jnp.float32)
        + lax.dot_general(up_grad, w_up, contract_last, preferred_element_type=jnp.float32)
    ).astype(jnp.bfloat16)
    return (expert_out, token_part, hidden, gate_grad, up_grad)


def squeeze_live(rows_x, rows_dy):
    total_rows = rows_x.shape[0]
    padded_rows = -(-total_rows // BLOCK) * BLOCK
    is_live = jnp.any(rows_x != 0, axis=1)
    live_count = is_live.astype(jnp.int32)
    live_total = jnp.sum(live_count)
    placement = jnp.where(
        is_live, jnp.cumsum(live_count) - 1, live_total + jnp.cumsum(1 - live_count) - 1
    )
    source_row = (
        jnp.zeros((padded_rows,), jnp.int32)
        .at[placement]
        .set(jnp.arange(total_rows, dtype=jnp.int32))
    )
    keep_row = (jnp.arange(padded_rows) < live_total)[:, None]
    packed_x = jnp.where(keep_row, rows_x[source_row], jnp.zeros((), rows_x.dtype))
    packed_dy = jnp.where(keep_row, rows_dy[source_row], jnp.zeros((), rows_dy.dtype))
    return (packed_x, packed_dy, placement, live_total)


def run_expert(rows_x, rows_dy, weights):
    packed_x, packed_dy, placement, live_total = squeeze_live(rows_x, rows_dy)
    padded_rows, model_width = packed_x.shape
    hidden_units = weights.shape[2]
    block_total = (live_total + BLOCK - 1) // BLOCK

    def block_step(block_index, state_in):
        row_start = block_index * BLOCK
        x_block = lax.dynamic_slice_in_dim(packed_x, row_start, BLOCK, 0)
        dy_block = lax.dynamic_slice_in_dim(packed_dy, row_start, BLOCK, 0)
        results = expert_rows(x_block, dy_block, weights)
        return tuple(
            (
                lax.dynamic_update_slice_in_dim(full_array, block_part, row_start, 0)
                for full_array, block_part in zip(state_in, results)
            )
        )

    initial = (
        jnp.zeros((padded_rows, model_width), jnp.bfloat16),
        jnp.zeros((padded_rows, model_width), jnp.bfloat16),
        jnp.zeros((padded_rows, hidden_units), jnp.bfloat16),
        jnp.zeros((padded_rows, hidden_units), jnp.bfloat16),
        jnp.zeros((padded_rows, hidden_units), jnp.bfloat16),
    )
    out_all, part_all, hidden_all, gate_all, up_all = lax.fori_loop(
        0, block_total, block_step, initial
    )
    contract_first = (((0,), (0,)), ((), ()))
    gate_term = lax.dot_general(
        packed_x, gate_all, contract_first, preferred_element_type=jnp.float32
    )
    up_term = lax.dot_general(packed_x, up_all, contract_first, preferred_element_type=jnp.float32)
    down_term = lax.dot_general(
        packed_dy, hidden_all, contract_first, preferred_element_type=jnp.float32
    )
    summed = lax.psum_scatter(
        jnp.stack([gate_term, up_term, down_term], axis=1)[:, None, :, :],
        "dp",
        scatter_dimension=0,
        tiled=True,
    )
    return (out_all[placement], part_all[placement], summed)


def per_device(tokens, expert_ids, gate_probs, cotangent, expert_weights):
    tok_rows, model_width = tokens.shape
    top_count = expert_ids.shape[1]
    held_count = lax.axis_size("expert")
    slot_total = held_count * CAP
    flat_ids = expert_ids.reshape(-1)
    is_held = flat_ids < held_count
    onehot = (flat_ids[:, None] == jnp.arange(held_count, dtype=jnp.int32)[None, :]).astype(
        jnp.int32
    )
    position = jnp.sum(jnp.cumsum(onehot, axis=0) * onehot, axis=1) - 1
    destination = jnp.where(is_held, flat_ids * CAP + position, slot_total)
    source_token = jnp.arange(tok_rows * top_count, dtype=jnp.int32) // top_count
    slot_token = jnp.zeros((slot_total,), jnp.int32).at[destination].set(source_token, mode="drop")
    slot_prob = (
        jnp.zeros((slot_total,), jnp.float32)
        .at[destination]
        .set(gate_probs.reshape(-1), mode="drop")
    )
    slot_live = jnp.zeros((slot_total,), jnp.bool_).at[destination].set(True, mode="drop")
    send_x = jnp.where(slot_live[:, None], tokens[slot_token], jnp.zeros((), jnp.bfloat16))
    send_dy = (slot_prob[:, None] * cotangent[slot_token].astype(jnp.float32)).astype(jnp.bfloat16)
    recv_x, recv_dy = (
        lax.all_to_all(
            send_x.reshape(held_count, CAP, model_width),
            "expert",
            split_axis=0,
            concat_axis=0,
            tiled=True,
        ),
        lax.all_to_all(
            send_dy.reshape(held_count, CAP, model_width),
            "expert",
            split_axis=0,
            concat_axis=0,
            tiled=True,
        ),
    )
    rows_x = recv_x.reshape(slot_total, model_width)
    rows_dy = recv_dy.reshape(slot_total, model_width)
    weights = expert_weights[:, 0]
    out_rows, part_rows, summed = run_expert(rows_x, rows_dy, weights)
    back_out, back_part = (
        lax.all_to_all(
            out_rows.reshape(held_count, CAP, model_width),
            "expert",
            split_axis=0,
            concat_axis=0,
            tiled=True,
        ),
        lax.all_to_all(
            part_rows.reshape(held_count, CAP, model_width),
            "expert",
            split_axis=0,
            concat_axis=0,
            tiled=True,
        ),
    )
    safe_slot = jnp.where(is_held, destination, 0)
    took_out = jnp.where(
        is_held[:, None],
        back_out.reshape(slot_total, model_width)[safe_slot].astype(jnp.float32),
        jnp.zeros((), jnp.float32),
    ).reshape(tok_rows, top_count, model_width)
    took_part = jnp.where(
        is_held[:, None],
        back_part.reshape(slot_total, model_width)[safe_slot].astype(jnp.float32),
        jnp.zeros((), jnp.float32),
    ).reshape(tok_rows, top_count, model_width)
    mixed_out = jnp.sum(gate_probs[:, :, None] * took_out, axis=1).astype(jnp.bfloat16)
    grad_gates = jnp.sum(took_out * cotangent.astype(jnp.float32)[:, None, :], axis=2)
    grad_tokens = jnp.sum(took_part, axis=1).astype(jnp.bfloat16)
    return (mixed_out, grad_tokens, grad_gates, summed.astype(jnp.bfloat16))


def solution(mesh):
    in_specs = (
        P(("dp", "expert"), None),
        P(("dp", "expert"), None),
        P(("dp", "expert"), None),
        P(("dp", "expert"), None),
        P(None, "expert", None, None),
    )
    out_specs = (
        P(("dp", "expert"), None),
        P(("dp", "expert"), None),
        P(("dp", "expert"), None),
        P("dp", "expert", None, None),
    )
    return jax.shard_map(
        per_device, mesh=mesh, in_specs=in_specs, out_specs=out_specs, check_vma=False
    )
```

profile of v0, /device:TPU:18, one launch (start us, length us, event | category | flops | bytes accessed | tf_op | source)
XLA Modules:
  0.0 269.7 jit_solution(8039451024025736921)
XLA Ops:
  7.2 0.8 broadcast_compare_fusion
  7.9 0.7 broadcast_multiply_fusion
  8.6 0.8 copy.18
  10.0 4.5 %reduce-window.24 = s32[16,8,128]{2,1,0:T(8,128)S(1)} reduce-window(s32[16,8,128]{2,1,0:T(8,128)S(1)} %fusion.49, s32[]{:T(128)} %constant.68.clone.1), window={size=1x1x128 pad=0_0x0_0x127_0}, to_apply=%region_0.0 | reduce-window | flops 2080768 | bytes 131076 | tf_op jit(solution)/shard_map/reduce-window
  15.0 4.3 %scatter_custom_fusion.1 = s32[384]{0:T(512)S(1)} fusion(s32[1024]{0:T(1024)S(1)} %bitcast.132, s32[1024]{0:T(1024)S(1)} %add_select_fusion, s32[]{:T(128)} %constant.68.clone.1), kind=kCustom, calls=%fused_computation.108 | custom fusion | bytes 1540 | tf_op jit(solution)/shard_map/scatter | solution.py:113
  19.4 4.3 %scatter_custom_fusion = pred[384]{0:T(512)(128)(4,1)S(1)} fusion(s32[1024]{0:T(1024)S(1)} %bitcast.133, pred[1024]{0:T(1024)(128)(4,1)S(1)} %broadcast.245, pred[]{:T(512)} %constant.70.clone.1), kind=kCustom, calls=%fused_computation.110 | custom fusion | bytes 385 | tf_op jit(solution)/shard_map/scatter | solution.py:119
  23.8 2.5 gather_fusion
  26.3 1.3 broadcast_select_fusion.2
  27.6 7.4 %all-to-all-start = ((bf16[16,24,2048]{2,1,0:T(8,128)(2,1)}), bf16[16,24,2048]{2,1,0:T(8,128)(2,1)S(1)}, u32[]{:S(2)}, u32[]{:S(2)}) async-start(bf16[16,24,2048]{2,1,0:T(8,128)(2,1)} %broadcast_select_fusion.2), calls=%async_computation | async-start | bytes 3145728 | tf_op jit(solution)/shard_map/all_to_all | solution.py:123
  35.2 4.3 %scatter_custom_fusion.3 = f32[384]{0:T(512)S(1)} fusion(s32[1024]{0:T(1024)S(1)} %bitcast.134, f32[1024]{0:T(1024)S(1)} %reshape.382, f32[]{:T(128)} %constant.80.clone.1), kind=kCustom, calls=%fused_computation.103 | custom fusion | bytes 1540 | tf_op jit(solution)/shard_map/scatter | solution.py:117
  39.6 3.1 %gather_fusion.2 = bf16[384,2048]{1,0:T(8,128)(2,1)} fusion(bf16[128,2048]{1,0:T(8,128)(2,1)S(1)} %copy-done.2, s32[1024]{0:T(1024)S(1)} %pad_clamp_fusion.2), kind=kCustom, calls=%fused_computation.2 | custom fusion | bytes 3147264 | tf_op jit(solution)/shard_map/gather | solution.py:121
  42.7 2.9 %fusion.46 = bf16[16,24,2048]{2,1,0:T(8,128)(2,1)} fusion(bf16[16,24,2048]{2,1,0:T(8,128)(2,1)} %bitcast.126, f32[16,24]{1,0:T(8,128)S(1)} %mul.84), kind=kLoop, calls=%fused_computation.63 | loop fusion | flops 2359296 | bytes 3147264 | tf_op jit(solution)/shard_map/convert_element_type | solution.py:121
  45.6 9.7 %all-to-all-done = bf16[16,24,2048]{2,1,0:T(8,128)(2,1)S(1)} async-done(((bf16[16,24,2048]{2,1,0:T(8,128)(2,1)}), bf16[16,24,2048]{2,1,0:T(8,128)(2,1)S(1)}, u32[]{:S(2)}, u32[]{:S(2)}) %all-to-all-start) | async-done | bytes 1572896 | tf_op jit(solution)/shard_map/all_to_all | solution.py:123
  55.3 7.8 %all-to-all-start.1 = ((bf16[16,24,2048]{2,1,0:T(8,128)(2,1)}), bf16[16,24,2048]{2,1,0:T(8,128)(2,1)}, u32[]{:S(2)}, u32[]{:S(2)}) async-start(bf16[16,24,2048]{2,1,0:T(8,128)(2,1)} %fusion.46), calls=%async_computation.1 | async-start | bytes 3145728 | tf_op jit(solution)/shard_map/all_to_all | solution.py:130
  66.4 0.7 add_bitcast_fusion
  67.1 2.9 %scatter_custom_fusion.2 = s32[384]{0:T(512)S(1)} fusion(s32[384]{0:T(512)S(1)} %fusion.53, s32[384]{0:T(512)S(1)} %iota.21, s32[]{:T(128)} %constant.68.clone.1), kind=kCustom, calls=%fused_computation.106 | custom fusion | bytes 1540 | tf_op jit(solution)/shard_map/scatter | solution.py:47
  70.7 10.6 %all-to-all-done.1 = bf16[16,24,2048]{2,1,0:T(8,128)(2,1)} async-done(((bf16[16,24,2048]{2,1,0:T(8,128)(2,1)}), bf16[16,24,2048]{2,1,0:T(8,128)(2,1)}, u32[]{:S(2)}, u32[]{:S(2)}) %all-to-all-start.1) | async-done | bytes 1572896 | tf_op jit(solution)/shard_map/all_to_all | solution.py:130
  81.3 6.7 %gather_fusion.3 = bf16[384,2048]{1,0:T(8,128)(2,1)} fusion(bf16[384,2048]{1,0:T(8,128)(2,1)} %bitcast.11, s32[1024]{0:T(1024)S(1)} %pad_clamp_fusion.1), kind=kCustom, calls=%fused_computation.3 | custom fusion | bytes 3147264 | tf_op jit(solution)/shard_map/gather | solution.py:51
  88.0 3.1 %gather_fusion.1 = bf16[384,2048]{1,0:T(8,128)(2,1)} fusion(bf16[384,2048]{1,0:T(8,128)(2,1)S(1)} %bitcast.122, s32[1024]{0:T(1024)S(1)} %pad_clamp_fusion.1), kind=kCustom, calls=%fused_computation.1 | custom fusion | bytes 3147264 | tf_op jit(solution)/shard_map/gather | solution.py:50
  91.1 3.8 %broadcast_select_fusion = (bf16[384,2048]{1,0:T(8,128)(2,1)}, bf16[384,2048]{1,0:T(8,128)(2,1)}) fusion(bf16[384,2048]{1,0:T(8,128)(2,1)} %gather_fusion.3, pred[384]{0:T(512)(128)(4,1)S(1)} %iota_compare_fusion.2, bf16[384,2048]{1,0:T(8,128)(2,1)} %gather_fusion.1), kind=kLoop, calls=%fused_computation.65 | loop fusion | flops 1572864 | bytes 6291840 | tf_op jit(solution)/shard_map/jit(_where)/select_n | solution.py:51
  94.9 0.8 broadcast.229.clone.1
  95.8 0.8 broadcast.229.clone
  96.6 0.9 broadcast.229
  97.8 12.3 %while.18 = (s32[]{:T(128)}, bf16[384,2048]{1,0:T(8,128)(2,1)S(1)}, bf16[384,2048]{1,0:T(8,128)(2,1)S(1)}, bf16[384,768]{1,0:T(8,128)(2,1)}, bf16[384,768]{1,0:T...) while((s32[]{:T(128)}, bf16[384,2048]{1,0:T(8,128)(2,1)S(1)}, ...), condition=%wide.region_14.15_spmd, body=%wide.region_13.14_spmd.sunk | while | flops 2418180096 | bytes 64685280 | solution.py:80
  97.9 2.8 %fusion.96 = f32[128,768]{1,0:T(8,128)S(1)} fusion(bf16[2048,3,768]{2,0,1:T(8,128)(2,1)} %get-tuple-element.218, bf16[384,2048]{1,0:T(8,128)(2,1)} %get-tuple-element.219, s32[]{:T(128)S(6)} %select_n.173), kind=kOutput, calls=%fused_computation.12.clone.1 | convolution fusion | flops 402653184 | bytes 4063236 | tf_op jit(solution)/shard_map/while/body/dot_general | solution.py:23
  100.7 3.1 %fusion.97 = f32[128,768]{1,0:T(8,128)S(1)} fusion(bf16[2048,3,768]{2,0,1:T(8,128)(2,1)} %get-tuple-element.218, bf16[384,2048]{1,0:T(8,128)(2,1)} %get-tuple-element.217, s32[]{:T(128)S(6)} %select_n.173), kind=kOutput, calls=%fused_computation.18.clone.1 | convolution fusion | flops 402653184 | bytes 4063236 | tf_op jit(solution)/shard_map/while/body/dot_general | solution.py:16
  103.8 2.6 constant_dynamic-update-slice_fusion.4
  106.5 1.1 fusion.99
  107.6 1.1 fusion.100
  108.7 1.1 fusion.98
  110.1 3.5 %convolution_bitcast_fusion.1 = f32[2048,1,768]{2,0,1:T(8,128)S(1)} fusion(bf16[384,2048]{1,0:T(8,128)(2,1)} %get-tuple-element.230, bf16[384,768]{1,0:T(8,128)(2,1)} %get-tuple-element.64), kind=kOutput, calls=%fused_computation.60 | convolution fusion | flops 1207959552 | bytes 8454144 | tf_op jit(solution)/shard_map/dot_general | solution.py:87
  113.7 1.8 convolution_bitcast_fusion.2
  115.6 1.8 convolution_bitcast_fusion
  117.4 6.7 %maximum_bitcast_fusion = f32[2048,1,3,768]{3,0,2,1:T(8,128)} fusion(f32[2048,1,768]{2,0,1:T(8,128)S(1)} %convolution_bitcast_fusion, f32[2048,1,768]{2,0,1:T(8,128)S(1)} %convolution_bitcast_fusion.1, f32[2048,1,768]{2,0,1:T(8,128)S(1)} %convolution_bitcast_fusion.2), kind=kLoop, calls=%fused_computation.49 | loop fusion | flops 9437184 | bytes 37748736 | tf_op jit(solution)/shard_map/broadcast_in_dim | solution.py:92
  124.2 3.1 %gather_fusion.4 = bf16[384,2048]{1,0:T(8,128)(2,1)} fusion(bf16[384,2048]{1,0:T(8,128)(2,1)S(1)} %get-tuple-element.61, s32[1024]{0:T(1024)S(1)} %pad_clamp_fusion), kind=kCustom, calls=%fused_computation.4 | custom fusion | bytes 3147264 | tf_op jit(solution)/shard_map/gather | solution.py:97
  127.3 28.8 %all-to-all-start.2 = ((bf16[16,24,2048]{2,1,0:T(8,128)(2,1)}), bf16[16,24,2048]{2,1,0:T(8,128)(2,1)S(1)}, u32[]{:S(2)}, u32[]{:S(2)}) async-start(bf16[16,24,2048]{2,1,0:T(8,128)(2,1)} %bitcast.125), calls=%async_computation.2 | async-start | bytes 3145728 | tf_op jit(solution)/shard_map/all_to_all | solution.py:143
  156.0 3.1 %gather_fusion.6 = bf16[384,2048]{1,0:T(8,128)(2,1)} fusion(bf16[384,2048]{1,0:T(8,128)(2,1)S(1)} %get-tuple-element.62, s32[1024]{0:T(1024)S(1)} %pad_clamp_fusion), kind=kCustom, calls=%fused_computation.6 | custom fusion | bytes 3147264 | tf_op jit(solution)/shard_map/gather | solution.py:97
  159.1 16.5 %all-to-all-done.2 = bf16[16,24,2048]{2,1,0:T(8,128)(2,1)S(1)} async-done(((bf16[16,24,2048]{2,1,0:T(8,128)(2,1)}), bf16[16,24,2048]{2,1,0:T(8,128)(2,1)S(1)}, u32[]{:S(2)}, u32[]{:S(2)}) %all-to-all-start.2) | async-done | bytes 1572896 | tf_op jit(solution)/shard_map/all_to_all | solution.py:143
  175.6 7.4 %all-to-all-start.3 = ((bf16[16,24,2048]{2,1,0:T(8,128)(2,1)}), bf16[16,24,2048]{2,1,0:T(8,128)(2,1)S(1)}, u32[]{:S(2)}, u32[]{:S(2)}) async-start(bf16[16,24,2048]{2,1,0:T(8,128)(2,1)} %bitcast.124), calls=%async_computation.3 | async-start | bytes 3145728 | tf_op jit(solution)/shard_map/all_to_all | solution.py:150
  183.1 2.2 convert_element_type.87
  185.4 6.0 %gather_fusion.5 = bf16[1024,2048]{1,0:T(8,128)(2,1)} fusion(bf16[384,2048]{1,0:T(8,128)(2,1)S(1)} %bitcast.120, s32[1024]{0:T(1024)S(1)} %broadcast_clamp_fusion), kind=kCustom, calls=%fused_computation.5 | custom fusion | bytes 8392704 | tf_op jit(solution)/shard_map/gather | solution.py:161
  191.4 3.4 %fusion.44 = f32[1024]{0:T(1024)S(1)} fusion(bf16[1024,2048]{1,0:T(8,128)(2,1)} %gather_fusion.5, f32[128,2048]{1,0:T(8,128)} %convert_element_type.87, pred[1024]{0:T(1024)(128)(4,1)S(1)} %broadcast_in_dim.96), kind=kLoop, calls=%fused_computation.56 | loop fusion | flops 8387584 | bytes 5248000 | tf_op jit(solution)/shard_map/reduce_sum | solution.py:170
  194.8 0.7 copy.24
  195.5 5.3 %all-to-all-done.3 = bf16[16,24,2048]{2,1,0:T(8,128)(2,1)S(1)} async-done(((bf16[16,24,2048]{2,1,0:T(8,128)(2,1)}), bf16[16,24,2048]{2,1,0:T(8,128)(2,1)S(1)}, u32[]{:S(2)}, u32[]{:S(2)}) %all-to-all-start.3) | async-done | bytes 1572896 | tf_op jit(solution)/shard_map/all_to_all | solution.py:150
  200.8 6.1 %gather_fusion.7 = bf16[1024,2048]{1,0:T(8,128)(2,1)} fusion(bf16[384,2048]{1,0:T(8,128)(2,1)S(1)} %bitcast.121, s32[1024]{0:T(1024)S(1)} %broadcast_clamp_fusion), kind=kCustom, calls=%fused_computation.7 | custom fusion | bytes 8392704 | tf_op jit(solution)/shard_map/gather | solution.py:166
  206.9 10.5 %fusion.45 = (bf16[128,2048]{1,0:T(8,128)(2,1)}, bf16[128,2048]{1,0:T(8,128)(2,1)}) fusion(bf16[1024,2048]{1,0:T(8,128)(2,1)} %gather_fusion.7, pred[128,8]{1,0:T(8,128)(4,1)S(1)} %copy.15, bf16[1024,2048]{1,0:T(8,128)(2,1)} %gather_fusion.5, f32[128,8]{1,0:T(8,128)S(1)} %copy.14), kind=kLoop, calls=%fused_computation.58 | loop fusion | flops 14155776 | bytes 9442304 | tf_op jit(solution)/shard_map/reduce_sum | solution.py:171
  217.4 43.3 %reduce-scatter.2.cloned.1.call-done = f32[128,1,3,768]{3,0,2,1:T(8,128)} async-done(((f32[2048,1,3,768]{3,0,2,1:T(8,128)}), f32[128,1,3,768]{3,0,2,1:T(8,128)}) %reduce-scatter.2.cloned.1.call-update) | async-done | bytes 1179664 | tf_op jit(solution)/shard_map/reduce_scatter | solution.py:91
  260.7 2.1 convert_element_type.88
  (69 shorter events, 5.4 us)
Async XLA Ops:
  7.2 16.7 %copy-start = (bf16[128,2048]{1,0:T(8,128)(2,1)S(1)}, bf16[128,2048]{1,0:T(8,128)(2,1)}, u32[]{:S(2)}) copy-start(bf16[128,2048]{1,0:T(8,128)(2,1)} %param.7) | copy-start | bytes 1572868
  27.6 7.4 %copy-start.8 = (f32[128,8]{0,1:T(8,128)S(1)}, f32[128,8]{0,1:T(8,128)}, u32[]{:S(2)}) copy-start(f32[128,8]{0,1:T(8,128)} %param.9) | copy-start | bytes 12292
  27.6 12.0 %copy-start.2 = (bf16[128,2048]{1,0:T(8,128)(2,1)S(1)}, bf16[128,2048]{1,0:T(8,128)(2,1)}, u32[]{:S(2)}) copy-start(bf16[128,2048]{1,0:T(8,128)(2,1)} %param.10) | copy-start | bytes 1572868
  27.6 27.6 %all-to-all-start = ((bf16[16,24,2048]{2,1,0:T(8,128)(2,1)}), bf16[16,24,2048]{2,1,0:T(8,128)(2,1)S(1)}, u32[]{:S(2)}, u32[]{:S(2)}) async-start(bf16[16,24,2048]{2,1,0:T(8,128)(2,1)} %broadcast_select_fusion.2), calls=%async_computation | async-start | bytes 3145728 | tf_op jit(solution)/shard_map/all_to_all | solution.py:123
  55.3 26.0 %all-to-all-start.1 = ((bf16[16,24,2048]{2,1,0:T(8,128)(2,1)}), bf16[16,24,2048]{2,1,0:T(8,128)(2,1)}, u32[]{:S(2)}, u32[]{:S(2)}) async-start(bf16[16,24,2048]{2,1,0:T(8,128)(2,1)} %fusion.46), calls=%async_computation.1 | async-start | bytes 3145728 | tf_op jit(solution)/shard_map/all_to_all | solution.py:130
  63.1 197.6 %reduce-scatter.2.cloned.1.call-start = ((), (), s32[]{:S(2)}) async-start(), calls=%async_computation.5 | async-start | bytes 20054016 | tf_op jit(solution)/shard_map/reduce_scatter | solution.py:91
  97.9 5.9 %copy-start.3 = (bf16[2048,3,768]{2,0,1:T(8,128)(2,1)S(1)}, bf16[2048,3,768]{2,0,1:T(8,128)(2,1)}, u32[]{:S(2)}) copy-start(bf16[2048,3,768]{2,0,1:T(8,128)(2,1)} %get-tuple-element.218) | copy-start | bytes 28311556 | tf_op jit(solution)/shard_map/while
  110.1 3.6 %copy-start.4 = (bf16[384,2048]{1,0:T(8,128)(2,1)S(1)}, bf16[384,2048]{1,0:T(8,128)(2,1)}, u32[]{:S(2)}) copy-start(bf16[384,2048]{1,0:T(8,128)(2,1)} %get-tuple-element.230) | copy-start | bytes 4718596
  110.1 3.6 %copy-start.6 = (bf16[384,768]{1,0:T(8,128)(2,1)S(1)}, bf16[384,768]{1,0:T(8,128)(2,1)}, u32[]{:S(2)}) copy-start(bf16[384,768]{1,0:T(8,128)(2,1)} %get-tuple-element.63) | copy-start | bytes 1769476
  113.7 1.9 copy-start.5
  113.7 1.9 copy-start.7
  127.3 48.4 %all-to-all-start.2 = ((bf16[16,24,2048]{2,1,0:T(8,128)(2,1)}), bf16[16,24,2048]{2,1,0:T(8,128)(2,1)S(1)}, u32[]{:S(2)}, u32[]{:S(2)}) async-start(bf16[16,24,2048]{2,1,0:T(8,128)(2,1)} %bitcast.125), calls=%async_computation.2 | async-start | bytes 3145728 | tf_op jit(solution)/shard_map/all_to_all | solution.py:143
  175.6 25.2 %all-to-all-start.3 = ((bf16[16,24,2048]{2,1,0:T(8,128)(2,1)}), bf16[16,24,2048]{2,1,0:T(8,128)(2,1)S(1)}, u32[]{:S(2)}, u32[]{:S(2)}) async-start(bf16[16,24,2048]{2,1,0:T(8,128)(2,1)} %bitcast.124), calls=%async_computation.3 | async-start | bytes 3145728 | tf_op jit(solution)/shard_map/all_to_all | solution.py:150
  206.9 56.0 %copy-start.1 = (bf16[128,2048]{1,0:T(8,128)(2,1)S(1)}, bf16[128,2048]{1,0:T(8,128)(2,1)}, u32[]{:S(2)}) copy-start(bf16[128,2048]{1,0:T(8,128)(2,1)} %param.7) | copy-start | bytes 1572868
Sparse Core Ops, SparseCore 0:
  124.3 136.3 reduce-scatter.1
where the time goes:
time: 270 us
  waiting for transfers between devices  85.4 us (32%)
  local copies, waits for them, and re-layouts  55.9 us (21%)
  starting transfers between devices  51.5 us (19%)
  other arithmetic  42.4 us (16%)
  matrix products  19.2 us (7%)
  between operations  15 us (6%)
    reduce_scatter x1, waiting for transfers between devices, run_expert(): lax.psum_scatter(jnp.stack([gate_term, up_term, down_term], axis=1)[:, No...  43.3 us
    all_to_all x1, starting transfers between devices, per_device(): lax.all_to_all(out_rows.reshape(held_count, CAP, model_width), 'expert',...  28.8 us
    all_to_all x1, waiting for transfers between devices, per_device(): lax.all_to_all(out_rows.reshape(held_count, CAP, model_width), 'expert',...  16.5 us
    all_to_all x1, waiting for transfers between devices, per_device(): lax.all_to_all(send_dy.reshape(held_count, CAP, model_width), 'expert', s...  10.6 us
    reduce_sum x1, other arithmetic, per_device(): grad_tokens = jnp.sum(took_part, axis=1).astype(jnp.bfloat16)  10.5 us
    all_to_all x1, waiting for transfers between devices, per_device(): lax.all_to_all(send_x.reshape(held_count, CAP, model_width), 'expert', sp...  9.66 us
    all_to_all x1, starting transfers between devices, per_device(): lax.all_to_all(send_dy.reshape(held_count, CAP, model_width), 'expert', s...  7.78 us
    all_to_all x1, starting transfers between devices, per_device(): lax.all_to_all(send_x.reshape(held_count, CAP, model_width), 'expert', sp...  7.38 us
  transfers between devices with their start and end apart: 5, of which 5 were waited for; matrix products, arithmetic and copies ran while one was open for 19% of the time, Pallas kernels for 0%

commit v1 on v0

v1 whole, which is shorter than its diff:
```python
import jax
import jax.numpy as jnp
from jax import lax
from jax.experimental import pallas as pl
from jax.experimental.pallas import tpu as pltpu
from jax.sharding import PartitionSpec as P

CAP = 24
TOK = 128
D = 2048
HALF = 1024
FF = 768
TOPK = 8
NX, NY, NZ = 4, 4, 8
HELD = NX * NY
BLK = 2 * CAP
PACK = HELD * BLK
ROWS = HELD * CAP
TILE = 256
CHUNK = D // (2 * NZ)
PIECE = CHUNK // 2
ORDER = (0, 1, 2)
BF16 = jnp.bfloat16
F32 = jnp.float32
NT = (((1,), (1,)), ((), ()))


def dot(a, b):
    return jnp.dot(a, b, preferred_element_type=F32)


def dot_nt(a, b):
    return lax.dot_general(a, b, NT, preferred_element_type=F32)


def moe_kernel(
    tok, ids, probs, cot, w_hbm,
    mixed, grad_tok, grad_gate, grad_w,
    w, onehot, prob, onehot_t, prob_hi, prob_lo, gate_acc,
    send_x, send_dy, recv_x, recv_dy, recv_out, recv_part,
    xs, dys, x_mine, x_other, dy_mine, dy_other, acts, silus, rights, grads,
    ring_send, ring_recv,
    w_sem, x_ss, x_rs, dy_ss, dy_rs, out_ss, out_rs, part_ss, part_rs,
    sib_ss, sib_rs, ring_ss, ring_rs,
):
    dp, ex = lax.axis_index("dp"), lax.axis_index("expert")
    z, core = lax.div(dp, 2), lax.rem(dp, 2)
    xx, yy = lax.div(ex, NY), lax.rem(ex, NY)

    def peer(i):
        px = lax.rem(xx + lax.div(i, NY), NX)
        py = lax.rem(yy + lax.rem(i, NY), NY)
        return px * NY + py

    sibling = {"dp": z * 2 + (1 - core), "expert": ex}
    after = {"dp": lax.rem(z + 1, NZ) * 2 + core, "expert": ex}
    before = {"dp": lax.rem(z + NZ - 1, NZ) * 2 + core, "expert": ex}

    w_copies = [pltpu.make_async_copy(w_hbm.at[m], w.at[m], w_sem.at[m]) for m in range(3)]
    for c in w_copies:
        c.start()

    barrier = pltpu.get_barrier_semaphore()

    def greet(i, _):
        pl.semaphore_signal(barrier, inc=1, device_id={"dp": dp, "expert": peer(i)})
        return 0

    lax.fori_loop(1, HELD, greet, 0)
    for other in (sibling, after, before):
        pl.semaphore_signal(barrier, inc=1, device_id=other)

    held_id = lax.broadcasted_iota(jnp.int32, (HELD, TOK), 0)
    has = jnp.zeros((HELD, TOK), F32)
    held_prob = jnp.zeros((HELD, TOK), F32)
    for k in range(TOPK):
        hit = ids[k : k + 1, :] == held_id
        has = jnp.where(hit, 1.0, has)
        held_prob = held_prob + jnp.where(hit, probs[k : k + 1, :], 0.0)
    earlier = lax.broadcasted_iota(jnp.int32, (TOK, TOK), 0) < lax.broadcasted_iota(
        jnp.int32, (TOK, TOK), 1
    )
    place = dot(has.astype(BF16), jnp.where(earlier, 1.0, 0.0).astype(BF16))
    place = jnp.where(has > 0.0, place, -1.0)
    slot = lax.broadcasted_iota(jnp.int32, (CAP, TOK), 0).astype(F32)
    zero = jnp.zeros((CAP, TOK), F32)
    for e in range(HELD):
        hit = place[e : e + 1, :] == slot
        one = jnp.where(hit, 1.0, 0.0)
        chance = jnp.where(hit, held_prob[e : e + 1, :], 0.0)
        low, mid, top = BLK * e, BLK * e + CAP, BLK * (e + 1)
        for ref, value in ((onehot, one), (prob, chance)):
            ref[low:mid, 0:TOK] = value
            ref[low:mid, TOK : 2 * TOK] = zero
            ref[mid:top, 0:TOK] = zero
            ref[mid:top, TOK : 2 * TOK] = value

    def columns(j):
        return pl.ds(pl.multiple_of(j * TILE, TILE), TILE)

    def stacked(ref, j):
        right = pl.ds(pl.multiple_of(HALF + j * TILE, TILE), TILE)
        return jnp.concatenate([ref[:, columns(j)], ref[:, right]], axis=0)

    def exchange(i, src, dst, send_sem, recv_sem):
        there = peer(i)
        return pltpu.make_async_remote_copy(
            src_ref=src.at[pl.ds(pl.multiple_of(there * BLK, BLK), BLK)],
            dst_ref=dst.at[pl.ds(pl.multiple_of(ex * BLK, BLK), BLK)],
            send_sem=send_sem.at[i],
            recv_sem=recv_sem.at[ex],
            device_id={"dp": dp, "expert": there},
        )

    def send_all(src, dst, send_sem, recv_sem):
        def one(i, _):
            exchange(i, src, dst, send_sem, recv_sem).start()
            return 0

        lax.fori_loop(1, HELD, one, 0)
        mine = pl.ds(pl.multiple_of(ex * BLK, BLK), BLK)
        pltpu.make_async_copy(src.at[mine], dst.at[mine], recv_sem.at[ex]).start()

    def wait_sent(src, dst, send_sem, recv_sem):
        def one(i, _):
            exchange(i, src, dst, send_sem, recv_sem).wait_send()
            return 0

        lax.fori_loop(1, HELD, one, 0)

    def wait_block(e, dst, recv_sem):
        rows = pl.ds(pl.multiple_of(e * BLK, BLK), BLK)
        pltpu.make_async_copy(dst.at[rows], dst.at[rows], recv_sem.at[e]).wait()

    def pack_x(j, _):
        send_x[:, columns(j)] = dot(onehot[...].astype(BF16), stacked(tok, j)).astype(BF16)
        return 0

    lax.fori_loop(0, HALF // TILE, pack_x, 0)
    pl.semaphore_wait(barrier, HELD - 1 + 3)
    send_all(send_x, recv_x, x_ss, x_rs)

    row_prob = jnp.sum(prob[...], axis=1, keepdims=True)

    def pack_dy(j, _):
        rows = dot(onehot[...].astype(BF16), stacked(cot, j))
        send_dy[:, columns(j)] = (row_prob * rows).astype(BF16)
        return 0

    lax.fori_loop(0, HALF // TILE, pack_dy, 0)
    send_all(send_dy, recv_dy, dy_ss, dy_rs)

    onehot_t[...] = jnp.transpose(onehot[...]).astype(BF16)
    prob_t = jnp.transpose(prob[...])
    high = prob_t.astype(BF16)
    prob_hi[...] = high
    prob_lo[...] = (prob_t - high.astype(F32)).astype(BF16)

    def unpack(recv, recv_sem, full):
        def one(i, _):
            wait_block(2 * i, recv, recv_sem)
            wait_block(2 * i + 1, recv, recv_sem)
            v = recv[pl.ds(pl.multiple_of(i * 2 * BLK, 2 * BLK), 2 * BLK), :].astype(F32)
            rows = pl.ds(pl.multiple_of(i * BLK, BLK), BLK)
            for h in range(2):
                parts = [v[CAP * (2 * b + h) : CAP * (2 * b + h + 1)] for b in range(2)]
                full[rows, HALF * h : HALF * (h + 1)] = jnp.concatenate(parts, axis=0).astype(BF16)
            return 0

        lax.fori_loop(0, HELD // 2, one, 0)

    def flip(full, mine, other):
        def one(c, _):
            at = pl.ds(pl.multiple_of(c * CHUNK, CHUNK), CHUNK)
            for ref, par in ((mine, core), (other, 1 - core)):
                cols = pl.ds(pl.multiple_of((2 * c + par) * CHUNK, CHUNK), CHUNK)
                ref[at, 0:ROWS] = jnp.transpose(full[:, cols])
            return 0

        lax.fori_loop(0, NZ, one, 0)

    def to_sibling(n, src, dst):
        return pltpu.make_async_remote_copy(
            src_ref=src, dst_ref=dst, send_sem=sib_ss.at[n], recv_sem=sib_rs.at[n], device_id=sibling
        )

    own, theirs = pl.ds(0, ROWS), pl.ds(ROWS, ROWS)
    sib = [to_sibling(m, rights.at[m, own], rights.at[m, theirs]) for m in range(3)]
    sib.append(to_sibling(3, x_other, x_mine.at[:, theirs]))
    sib.append(to_sibling(4, dy_other, dy_mine.at[:, theirs]))

    unpack(recv_x, x_rs, xs)
    w_copies[0].wait()
    w_copies[1].wait()

    def project(j, _):
        g = dot(xs[...], w[0, :, columns(j)])
        u = dot(xs[...], w[1, :, columns(j)])
        s = jax.nn.sigmoid(g)
        silu = g * s
        rights[2, own, columns(j)] = (silu * u).astype(BF16)
        acts[:, columns(j)] = u * s * (1.0 + g * (1.0 - s))
        silus[:, columns(j)] = silu
        return 0

    lax.fori_loop(0, FF // TILE, project, 0)
    sib[2].start()
    w_copies[2].wait()
    wait_sent(send_x, recv_x, x_ss, x_rs)

    def repack(ref, j, left, right):
        parts = []
        for s in range(HELD):
            parts += [left[CAP * s : CAP * (s + 1)], right[CAP * s : CAP * (s + 1)]]
        ref[:, columns(j)] = jnp.concatenate(parts, axis=0).astype(BF16)

    def features(j):
        first = pl.ds(pl.multiple_of(j * TILE, TILE), TILE)
        second = pl.ds(pl.multiple_of(HALF + j * TILE, TILE), TILE)
        return first, second

    def expert_out(j, _):
        hidden = rights[2, own, :]
        left, right = [dot_nt(hidden, w[2, rows, :]) for rows in features(j)]
        repack(send_x, j, left, right)
        return 0

    lax.fori_loop(0, HALF // TILE, expert_out, 0)
    flip(xs, x_mine, x_other)
    sib[3].start()

    unpack(recv_dy, dy_rs, dys)
    send_all(send_x, recv_out, out_ss, out_rs)

    def hidden_grad(j, _):
        hg = dot(dys[...], w[2, :, columns(j)])
        rights[0, own, columns(j)] = (hg * acts[:, columns(j)]).astype(BF16)
        rights[1, own, columns(j)] = (hg * silus[:, columns(j)]).astype(BF16)
        return 0

    lax.fori_loop(0, FF // TILE, hidden_grad, 0)
    sib[0].start()
    sib[1].start()
    flip(dys, dy_mine, dy_other)
    sib[4].start()

    def piece(m, way, chunk):
        return grads[m, pl.ds(pl.multiple_of(chunk * CHUNK + way * PIECE, PIECE), PIECE), :]

    def ring(m, way, step):
        n = (step * 3 + m) * 2 + way
        return pltpu.make_async_remote_copy(
            src_ref=ring_send.at[n],
            dst_ref=ring_recv.at[n],
            send_sem=ring_ss.at[n],
            recv_sem=ring_rs.at[n],
            device_id=(after, before)[way],
        )

    def chunk_at(way, distance):
        return lax.rem(z + (NZ - distance if way == 0 else distance), NZ)

    sib[3].wait()
    sib[2].wait()
    for m in ORDER:
        if m < 2:
            sib[m].wait()
        else:
            sib[4].wait()
        lefts = x_mine if m < 2 else dy_mine

        def weight_grad(j, _, m=m, lefts=lefts):
            grads[m, :, columns(j)] = dot(lefts[...], rights[m, :, columns(j)])
            return 0

        lax.fori_loop(0, FF // TILE, weight_grad, 0)
        for way in range(2):
            ring_send[m * 2 + way] = piece(m, way, chunk_at(way, 1)).astype(BF16)
            ring(m, way, 0).start()

    wait_sent(send_dy, recv_dy, dy_ss, dy_rs)

    def token_part(j, _):
        gate_g, up_g = rights[0, own, :], rights[1, own, :]
        left, right = [
            dot_nt(gate_g, w[0, rows, :]) + dot_nt(up_g, w[1, rows, :]) for rows in features(j)
        ]
        repack(send_dy, j, left, right)
        return 0

    lax.fori_loop(0, HALF // TILE, token_part, 0)
    send_all(send_dy, recv_part, part_ss, part_rs)

    def pass_on(step, _):
        for m in ORDER:
            for way in range(2):
                ring(m, way, step).wait_recv()
                n = (step * 3 + m) * 2 + way
                total = ring_recv[n].astype(F32) + piece(m, way, chunk_at(way, step + 2))
                ring_send[n + 6] = total.astype(BF16)
                ring(m, way, step + 1).start()
        return 0

    lax.fori_loop(0, NZ - 2, pass_on, 0)

    def wait_out(e, _):
        wait_block(e, recv_out, out_rs)
        wait_block(e, recv_part, part_rs)
        return 0

    lax.fori_loop(0, HELD, wait_out, 0)
    gate_acc[...] = jnp.zeros_like(gate_acc)

    def combine(j, _):
        back = recv_out[:, columns(j)]
        first, second = features(j)
        mix = dot(prob_hi[...], back) + dot(prob_lo[...], back)
        mixed[:, first] = mix[0:TOK].astype(BF16)
        mixed[:, second] = mix[TOK : 2 * TOK].astype(BF16)
        tokens_g = dot(onehot_t[...], recv_part[:, columns(j)])
        grad_tok[:, first] = tokens_g[0:TOK].astype(BF16)
        grad_tok[:, second] = tokens_g[TOK : 2 * TOK].astype(BF16)
        product = back.astype(F32) * dot(onehot[...].astype(BF16), stacked(cot, j))
        gate_acc[...] += product[:, 0:TOK] + product[:, TOK : 2 * TOK]
        return 0

    lax.fori_loop(0, HALF // TILE, combine, 0)
    inner = jnp.sum(gate_acc[...], axis=1, keepdims=True) * onehot[...]
    result = jnp.zeros((TOPK, TOK), F32)
    for e in range(HELD):
        both = jnp.sum(inner[BLK * e : BLK * (e + 1)], axis=0, keepdims=True)
        value = both[:, 0:TOK] + both[:, TOK : 2 * TOK]
        result = jnp.where(ids[...] == e, value, result)
    grad_gate[...] = result

    for m in ORDER:
        for way in range(2):
            step = NZ - 2
            ring(m, way, step).wait_recv()
            n = (step * 3 + m) * 2 + way
            total = ring_recv[n].astype(F32) + piece(m, way, z)
            grad_w[m, PIECE * way : PIECE * (way + 1), :] = total.astype(BF16)

    wait_sent(send_x, recv_out, out_ss, out_rs)
    wait_sent(send_dy, recv_part, part_ss, part_rs)

    def wait_ring(step, _):
        for m in ORDER:
            for way in range(2):
                ring(m, way, step).wait_send()
        return 0

    lax.fori_loop(0, NZ - 1, wait_ring, 0)


def per_device(tokens, expert_ids, gate_probs, cotangent, expert_weights):
    weights = jnp.transpose(expert_weights[:, 0], (1, 0, 2))
    vmem = pl.BlockSpec(memory_space=pltpu.VMEM)
    pieces = (NZ - 1) * 6
    dma = pltpu.SemaphoreType.DMA
    mixed, grad_tok, grad_gate, grad_w = pl.pallas_call(
        moe_kernel,
        out_shape=(
            jax.ShapeDtypeStruct((TOK, D), BF16),
            jax.ShapeDtypeStruct((TOK, D), BF16),
            jax.ShapeDtypeStruct((TOPK, TOK), F32),
            jax.ShapeDtypeStruct((3, CHUNK, FF), BF16),
        ),
        in_specs=[vmem] * 4 + [pl.BlockSpec(memory_space=pl.ANY)],
        out_specs=(vmem,) * 4,
        scratch_shapes=[
            pltpu.VMEM((3, D, FF), BF16),
            pltpu.VMEM((PACK, 2 * TOK), F32),
            pltpu.VMEM((PACK, 2 * TOK), F32),
            pltpu.VMEM((2 * TOK, PACK), BF16),
            pltpu.VMEM((2 * TOK, PACK), BF16),
            pltpu.VMEM((2 * TOK, PACK), BF16),
            pltpu.VMEM((PACK, TOK), F32),
        ]
        + [pltpu.VMEM((PACK, HALF), BF16)] * 6
        + [pltpu.VMEM((ROWS, D), BF16)] * 2
        + [pltpu.VMEM((HALF, 2 * ROWS), BF16), pltpu.VMEM((HALF, ROWS), BF16)] * 2
        + [pltpu.VMEM((ROWS, FF), F32)] * 2
        + [pltpu.VMEM((3, 2 * ROWS, FF), BF16), pltpu.VMEM((3, HALF, FF), F32)]
        + [pltpu.VMEM((pieces, PIECE, FF), BF16)] * 2
        + [dma((3,))]
        + [dma((HELD,))] * 8
        + [dma((5,))] * 2
        + [dma((pieces,))] * 2,
        compiler_params=pltpu.CompilerParams(
            collective_id=0, has_side_effects=True, vmem_limit_bytes=60 << 20
        ),
    )(tokens, expert_ids.T, gate_probs.T, cotangent, weights)
    return mixed, grad_tok, grad_gate.T, jnp.transpose(grad_w, (1, 0, 2))[:, None]


def solution(mesh):
    rows = P(("dp", "expert"), None)
    return jax.shard_map(
        per_device,
        mesh=mesh,
        in_specs=(rows, rows, rows, rows, P(None, "expert", None, None)),
        out_specs=(rows, rows, rows, P("dp", "expert", None, None)),
        check_vma=False,
    )
```

time: 270 us -> 118 us (0.44)
  the two profiles are of different devices: /device:TPU:18 before, /device:TPU:28 now
where the time goes in v1:
time: 118 us
  Pallas kernels  110 us (93%)
  local copies, waits for them, and re-layouts  6.95 us (6%)
    pallas_call x1, Pallas kernels, per_device(): pl.pallas_call(moe_kernel, out_shape=(jax.ShapeDtypeStruct((TOK, D), BF16...  110 us
    unnamed x4, local copies, waits for them, and re-layouts  6.95 us

profile of v1, /device:TPU:28, one launch (start us, length us, event | category | flops | bytes accessed | tf_op | source)
XLA Modules:
  0.0 118.1 jit_solution(3143667401174796973)
XLA Ops:
  0.6 110.5 %shard_map.84 = (bf16[128,2048]{1,0:T(8,128)(2,1)}, bf16[128,2048]{1,0:T(8,128)(2,1)}, f32[8,128]{1,0:T(8,128)}, bf16[3,128,768]{2,1,0:T(8,128)(2,1)}) custom-call(bf16[128,2048]{1,0:T(8,128)(2,1)} %tok.1, s32[8,128]{1,0:T(8,128)} %bitcast.11, f32[8,128]{1,0:T(8,128)} %bitcast.12, bf16[128,2048]{1,0:T(8,128)(2,1)} %cot.1, bf16[3,2048,768]{2,1,0:T(8,128)(2,1)} %bitcast.9), custom_call_target="tpu_custom_call" | custom-call | tf_op jit(solution)/shard_map/pallas_call | solution.py:361
  111.1 1.9 %copy.13 = bf16[128,2048]{1,0:T(8,128)(2,1)} copy(bf16[128,2048]{1,0:T(8,128)(2,1)} %get-tuple-element.16) | data formatting | bytes 1048576
  113.0 1.9 %copy.14 = bf16[128,2048]{1,0:T(8,128)(2,1)} copy(bf16[128,2048]{1,0:T(8,128)(2,1)} %get-tuple-element.17) | data formatting | bytes 1048576
  114.9 1.3 %copy.15 = f32[128,8]{0,1:T(8,128)} copy(f32[128,8]{0,1:T(8,128)} %bitcast.13) | data formatting | bytes 8192
  116.2 1.9 %copy.16 = bf16[128,1,3,768]{3,0,2,1:T(8,128)(2,1)} copy(bf16[128,1,3,768]{3,0,2,1:T(8,128)(2,1)} %bitcast.10) | data formatting | bytes 1179648

commit v2 on v1

v2 whole, which is shorter than its diff:
```python
import jax
import jax.numpy as jnp
from jax import lax
from jax.experimental import pallas as pl
from jax.experimental.pallas import tpu as pltpu
from jax.sharding import PartitionSpec as P

CAP = 24
TOK = 128
D = 2048
HALF = 1024
FF = 768
TOPK = 8
NX, NY, NZ = 4, 4, 8
HELD = NX * NY
BLK = 2 * CAP
PACK = HELD * BLK
ROWS = HELD * CAP
TILE = 256
TILES = HALF // TILE
CHUNK = D // (2 * NZ)
PIECE = CHUNK // 2
HIDDEN_PIECE = FF // 2
ORDER = (2, 0, 1)
OFFSETS = (
    (0, 0), (0, 1), (1, 0), (0, 3), (3, 0), (0, 2), (2, 0), (1, 1),
    (3, 3), (1, 3), (3, 1), (2, 1), (1, 2), (2, 3), (3, 2), (2, 2),
)
BF16 = jnp.bfloat16
F32 = jnp.float32
NT = (((1,), (1,)), ((), ()))


def dot(a, b):
    return jnp.dot(a, b, preferred_element_type=F32)


def dot_nt(a, b):
    return lax.dot_general(a, b, NT, preferred_element_type=F32)


def moe_kernel(
    tok_hbm, ids_hbm, probs_hbm, cot_hbm, w_hbm,
    mixed, grad_tok, grad_gate, grad_w,
    tok, ids, probs, cot,
    w, place, held_prob, onehot, onehot_b, prob, onehot_t, prob_hi, prob_lo, gate_acc,
    send_x, send_dy, recv_x, recv_dy, recv_out, recv_part,
    xs, dys, x_mine, x_other, hidden, hidden_t, acts, silus, rights, grads, grads_t,
    ring_send, ring_recv, ring_send_t, ring_recv_t,
    in_sem, w_sem, x_ss, x_rs, dy_ss, dy_rs, out_ss, out_rs, part_ss, part_rs,
    sib_ss, sib_rs, ring_ss, ring_rs,
):
    dp, ex = lax.axis_index("dp"), lax.axis_index("expert")
    z, core = lax.div(dp, 2), lax.rem(dp, 2)
    xx, yy = lax.div(ex, NY), lax.rem(ex, NY)

    def peer(n, way=1):
        dx, dy = OFFSETS[n]
        if way < 0:
            dx, dy = (NX - dx) % NX, (NY - dy) % NY
        return lax.rem(xx + dx, NX) * NY + lax.rem(yy + dy, NY)

    sibling = {"dp": z * 2 + (1 - core), "expert": ex}
    after = {"dp": lax.rem(z + 1, NZ) * 2 + core, "expert": ex}
    before = {"dp": lax.rem(z + NZ - 1, NZ) * 2 + core, "expert": ex}

    loads = [
        pltpu.make_async_copy(src, dst, in_sem.at[n])
        for n, (src, dst) in enumerate(
            ((ids_hbm, ids), (probs_hbm, probs), (tok_hbm, tok), (cot_hbm, cot))
        )
    ]
    for c in loads:
        c.start()
    w_copies = [
        pltpu.make_async_copy(w_hbm.at[m, :, par], w.at[m, par], w_sem.at[2 * m + par])
        for m in range(3)
        for par in range(2)
    ]

    barrier = pltpu.get_barrier_semaphore()
    for n in range(1, HELD):
        pl.semaphore_signal(barrier, inc=1, device_id={"dp": dp, "expert": peer(n)})
    for other in (sibling, after, before):
        pl.semaphore_signal(barrier, inc=1, device_id=other)

    loads[0].wait()
    loads[1].wait()

    held_id = lax.broadcasted_iota(jnp.int32, (HELD, TOK), 0)
    has = jnp.zeros((HELD, TOK), F32)
    chances = jnp.zeros((HELD, TOK), F32)
    for k in range(TOPK):
        hit = ids[k : k + 1, :] == held_id
        has = jnp.where(hit, 1.0, has)
        chances = chances + jnp.where(hit, probs[k : k + 1, :], 0.0)
    held_prob[...] = chances
    earlier = lax.broadcasted_iota(jnp.int32, (TOK, TOK), 0) < lax.broadcasted_iota(
        jnp.int32, (TOK, TOK), 1
    )
    count = dot(has.astype(BF16), jnp.where(earlier, 1.0, 0.0).astype(BF16))
    place[...] = jnp.where(has > 0.0, count, -1.0)
    slot = lax.broadcasted_iota(jnp.int32, (CAP, TOK), 0).astype(F32)
    zero = jnp.zeros((CAP, TOK), F32)

    def fill(ref, n, value):
        low, mid, top = BLK * n, BLK * n + CAP, BLK * (n + 1)
        ref[low:mid, 0:TOK] = value
        ref[low:mid, TOK : 2 * TOK] = zero
        ref[mid:top, 0:TOK] = zero
        ref[mid:top, TOK : 2 * TOK] = value

    def hits(n):
        return place[pl.ds(peer(n), 1), :] == slot

    def chunk_columns(j, c, h):
        return pl.ds(pl.multiple_of((4 * j + 2 * c + h) * CHUNK, CHUNK), CHUNK)

    def stacked(ref, j):
        halves = [
            jnp.concatenate([ref[:, chunk_columns(j, c, h)] for c in range(2)], axis=1)
            for h in range(2)
        ]
        return jnp.concatenate(halves, axis=0)

    def columns(j):
        return pl.ds(pl.multiple_of(j * TILE, TILE), TILE)

    def exchange(n, way, src, dst, send_sem, recv_sem):
        rows = pl.ds(BLK * n, BLK)
        return pltpu.make_async_remote_copy(
            src_ref=src.at[rows],
            dst_ref=dst.at[rows],
            send_sem=send_sem.at[n],
            recv_sem=recv_sem.at[n],
            device_id={"dp": dp, "expert": peer(n, way)},
        )

    def send_blocks(blocks, way, src, dst, send_sem, recv_sem):
        for n in blocks:
            if n:
                exchange(n, way, src, dst, send_sem, recv_sem).start()
            else:
                mine = pl.ds(0, BLK)
                pltpu.make_async_copy(src.at[mine], dst.at[mine], recv_sem.at[0]).start()

    def wait_sent(way, src, dst, send_sem, recv_sem):
        for n in range(1, HELD):
            exchange(n, way, src, dst, send_sem, recv_sem).wait_send()

    def wait_block(n, dst, recv_sem):
        rows = pl.ds(pl.multiple_of(n * BLK, BLK), BLK)
        pltpu.make_async_copy(dst.at[rows], dst.at[rows], recv_sem.at[n]).wait()

    x_way = (send_x, recv_x, x_ss, x_rs)
    dy_way = (send_dy, recv_dy, dy_ss, dy_rs)
    out_way = (send_x, recv_out, out_ss, out_rs)
    part_way = (send_dy, recv_part, part_ss, part_rs)
    everyone = range(HELD)

    for group in range(2):
        blocks = range(HELD // 2 * group, HELD // 2 * (group + 1))
        for n in blocks:
            fill(onehot, n, jnp.where(hits(n), 1.0, 0.0))
        rows = pl.ds(PACK // 2 * group, PACK // 2)
        onehot_b[rows, :] = onehot[rows, :].astype(BF16)
        if group == 0:
            loads[2].wait()
            for c in w_copies:
                c.start()

        def pack_x(j, _, rows=rows):
            send_x[rows, columns(j)] = dot(onehot_b[rows, :], stacked(tok, j)).astype(BF16)
            return 0

        lax.fori_loop(0, TILES, pack_x, 0)
        if group == 0:
            pl.semaphore_wait(barrier, HELD - 1 + 3)
        send_blocks(blocks, 1, *x_way)

    for n in everyone:
        fill(prob, n, jnp.where(hits(n), held_prob[pl.ds(peer(n), 1), :], 0.0))
    row_prob = jnp.sum(prob[...], axis=1, keepdims=True)
    loads[3].wait()

    def pack_dy(j, _):
        picked = dot(onehot_b[...], stacked(cot, j))
        send_dy[:, columns(j)] = (row_prob * picked).astype(BF16)
        return 0

    lax.fori_loop(0, TILES, pack_dy, 0)
    send_blocks(everyone, 1, *dy_way)

    onehot_t[...] = jnp.transpose(onehot[...]).astype(BF16)
    prob_t = jnp.transpose(prob[...])
    high = prob_t.astype(BF16)
    prob_hi[...] = high
    prob_lo[...] = (prob_t - high.astype(F32)).astype(BF16)

    own, theirs = pl.ds(0, ROWS), pl.ds(ROWS, ROWS)

    def to_sibling(n, src, dst):
        return pltpu.make_async_remote_copy(
            src_ref=src, dst_ref=dst, send_sem=sib_ss.at[n], recv_sem=sib_rs.at[n], device_id=sibling
        )

    x_over = to_sibling(0, x_other, x_mine.at[:, theirs])
    hidden_over = to_sibling(1, hidden_t.at[:, own], hidden_t.at[:, theirs])

    def dy_over(i):
        rows = pl.ds(pl.multiple_of(i * BLK, BLK), BLK)
        there = pl.ds(pl.multiple_of(ROWS + i * BLK, BLK), BLK)
        return to_sibling(2 + i, dys.at[1 - core, rows], dys.at[1 - core, there])

    def grad_over(m, j):
        src, dst = rights.at[m, own, columns(j)], rights.at[m, theirs, columns(j)]
        return to_sibling(2 + HELD // 2 + 3 * m + j, src, dst)

    def unpack(recv, recv_sem, full, then=None):
        def one(i, _):
            wait_block(2 * i, recv, recv_sem)
            wait_block(2 * i + 1, recv, recv_sem)
            v = recv[pl.ds(pl.multiple_of(i * 2 * BLK, 2 * BLK), 2 * BLK), :].astype(F32)
            rows = pl.ds(pl.multiple_of(i * BLK, BLK), BLK)
            for h in range(2):
                parts = [v[CAP * (2 * b + h) : CAP * (2 * b + h + 1)] for b in range(2)]
                full[h, rows, :] = jnp.concatenate(parts, axis=0).astype(BF16)
            if then is not None:
                then(i).start()
            return 0

        lax.fori_loop(0, HELD // 2, one, 0)

    def weight(m, h, j):
        return w[m, h, :, :, columns(j)].reshape(HALF, TILE)

    unpack(recv_x, x_rs, xs)
    for c in w_copies:
        c.wait()

    def project(j, _):
        g = dot(xs[0], weight(0, 0, j)) + dot(xs[1], weight(0, 1, j))
        u = dot(xs[0], weight(1, 0, j)) + dot(xs[1], weight(1, 1, j))
        s = jax.nn.sigmoid(g)
        silu = g * s
        units = (silu * u).astype(BF16)
        hidden[:, columns(j)] = units
        hidden_t[columns(j), own] = jnp.transpose(units)
        acts[:, columns(j)] = u * s * (1.0 + g * (1.0 - s))
        silus[:, columns(j)] = silu
        return 0

    lax.fori_loop(0, FF // TILE, project, 0)
    hidden_over.start()

    def flip(c, _):
        at = pl.ds(pl.multiple_of(c * CHUNK, CHUNK), CHUNK)
        x_mine[at, own] = jnp.transpose(xs[core, :, at])
        x_other[at, :] = jnp.transpose(xs[1 - core, :, at])
        return 0

    lax.fori_loop(0, NZ, flip, 0)
    x_over.start()
    wait_sent(1, *x_way)

    def repack(ref, j, left, right):
        parts = []
        for n in range(HELD):
            parts += [left[CAP * n : CAP * (n + 1)], right[CAP * n : CAP * (n + 1)]]
        ref[:, columns(j)] = jnp.concatenate(parts, axis=0).astype(BF16)

    def weight_rows(m, h, j):
        return w[m, h, pl.ds(2 * j, 2)].reshape(TILE, FF)

    def expert_out(j, _):
        left, right = [dot_nt(hidden[...], weight_rows(2, h, j)) for h in range(2)]
        repack(send_x, j, left, right)
        return 0

    lax.fori_loop(0, TILES, expert_out, 0)
    unpack(recv_dy, dy_rs, dys, dy_over)
    send_blocks(everyone, -1, *out_way)

    for j in range(FF // TILE):
        hg = dot(dys[0, own, :], weight(2, 0, j)) + dot(dys[1, own, :], weight(2, 1, j))
        rights[0, own, columns(j)] = (hg * acts[:, columns(j)]).astype(BF16)
        rights[1, own, columns(j)] = (hg * silus[:, columns(j)]).astype(BF16)
        grad_over(0, j).start()
        grad_over(1, j).start()

    def piece(m, way, chunk):
        if m == 2:
            cols = pl.ds(pl.multiple_of(chunk * CHUNK, CHUNK), CHUNK)
            return grads_t[HIDDEN_PIECE * way : HIDDEN_PIECE * (way + 1), cols]
        return grads[m, pl.ds(pl.multiple_of(chunk * CHUNK + way * PIECE, PIECE), PIECE), :]

    def slots(m, way, step):
        if m == 2:
            return ring_send_t, ring_recv_t, step * 2 + way
        return ring_send, ring_recv, (step * 2 + m) * 2 + way

    def ring(m, way, step):
        src, dst, n = slots(m, way, step)
        k = (step * 3 + m) * 2 + way
        return pltpu.make_async_remote_copy(
            src_ref=src.at[n],
            dst_ref=dst.at[n],
            send_sem=ring_ss.at[k],
            recv_sem=ring_rs.at[k],
            device_id=(after, before)[way],
        )

    def chunk_at(way, distance):
        return lax.rem(z + (NZ - distance if way == 0 else distance), NZ)

    def begin(m):
        for way in range(2):
            src, _, n = slots(m, way, 0)
            src[n] = piece(m, way, chunk_at(way, 1)).astype(BF16)
            ring(m, way, 0).start()

    hidden_over.wait()
    for i in range(HELD // 2):
        dy_over(i).wait()

    def down_grad(j, _):
        grads_t[:, columns(j)] = dot(hidden_t[...], dys[core, :, columns(j)])
        return 0

    lax.fori_loop(0, TILES, down_grad, 0)
    begin(2)
    x_over.wait()
    for m in range(2):
        for j in range(FF // TILE):
            grad_over(m, j).wait()

        def weight_grad(j, _, m=m):
            grads[m, :, columns(j)] = dot(x_mine[...], rights[m, :, columns(j)])
            return 0

        lax.fori_loop(0, FF // TILE, weight_grad, 0)
        begin(m)

    wait_sent(1, *dy_way)

    def token_part(j, _):
        gate_g, up_g = rights[0, own, :], rights[1, own, :]
        left, right = [
            dot_nt(gate_g, weight_rows(0, h, j)) + dot_nt(up_g, weight_rows(1, h, j))
            for h in range(2)
        ]
        repack(send_dy, j, left, right)
        return 0

    lax.fori_loop(0, TILES, token_part, 0)
    send_blocks(everyone, -1, *part_way)

    def pass_on(step, _):
        for m in ORDER:
            for way in range(2):
                ring(m, way, step).wait_recv()
                src, dst, n = slots(m, way, step)
                total = dst[n].astype(F32) + piece(m, way, chunk_at(way, step + 2))
                src[n + (2 if m == 2 else 4)] = total.astype(BF16)
                ring(m, way, step + 1).start()
        return 0

    lax.fori_loop(0, NZ - 2, pass_on, 0)

    for n in everyone:
        wait_block(n, recv_out, out_rs)
        wait_block(n, recv_part, part_rs)
    gate_acc[...] = jnp.zeros_like(gate_acc)

    def spread(ref, j, value):
        for h in range(2):
            for c in range(2):
                ref[:, chunk_columns(j, c, h)] = value[
                    TOK * h : TOK * (h + 1), CHUNK * c : CHUNK * (c + 1)
                ].astype(BF16)

    def combine(j, _):
        back = recv_out[:, columns(j)]
        spread(mixed, j, dot(prob_hi[...], back) + dot(prob_lo[...], back))
        spread(grad_tok, j, dot(onehot_t[...], recv_part[:, columns(j)]))
        product = back.astype(F32) * dot(onehot_b[...], stacked(cot, j))
        gate_acc[...] += product[:, 0:TOK] + product[:, TOK : 2 * TOK]
        return 0

    lax.fori_loop(0, TILES, combine, 0)
    inner = jnp.sum(gate_acc[...], axis=1, keepdims=True) * onehot[...]
    result = jnp.zeros((TOPK, TOK), F32)
    for n in everyone:
        both = jnp.sum(inner[BLK * n : BLK * (n + 1)], axis=0, keepdims=True)
        value = both[:, 0:TOK] + both[:, TOK : 2 * TOK]
        result = jnp.where(ids[...] == peer(n), value, result)
    grad_gate[...] = result

    for m in ORDER:
        for way in range(2):
            ring(m, way, NZ - 2).wait_recv()
            _, dst, n = slots(m, way, NZ - 2)
            total = dst[n].astype(F32) + piece(m, way, z)
            if m == 2:
                cols = pl.ds(HIDDEN_PIECE * way, HIDDEN_PIECE)
                grad_w[m, :, cols] = jnp.transpose(total).astype(BF16)
            else:
                grad_w[m, PIECE * way : PIECE * (way + 1), :] = total.astype(BF16)

    wait_sent(-1, *out_way)
    wait_sent(-1, *part_way)

    def wait_ring(step, _):
        for m in ORDER:
            for way in range(2):
                ring(m, way, step).wait_send()
        return 0

    lax.fori_loop(0, NZ - 1, wait_ring, 0)


def hand_out(*refs):
    ins, outs, sem = refs[:4], refs[4:8], refs[8]
    copies = [pltpu.make_async_copy(a, b, sem.at[n]) for n, (a, b) in enumerate(zip(ins, outs))]
    for c in copies:
        c.start()
    for c in copies:
        c.wait()


def per_device(tokens, expert_ids, gate_probs, cotangent, expert_weights):
    weights = jnp.transpose(expert_weights[:, 0], (1, 0, 2)).reshape(3, NZ, 2, CHUNK, FF)
    anywhere = pl.BlockSpec(memory_space=pl.ANY)
    dma = pltpu.SemaphoreType.DMA
    vmem = pltpu.VMEM
    results = (
        jax.ShapeDtypeStruct((TOK, D), BF16),
        jax.ShapeDtypeStruct((TOK, D), BF16),
        jax.ShapeDtypeStruct((TOPK, TOK), F32),
        jax.ShapeDtypeStruct((3, CHUNK, FF), BF16),
    )
    made = pl.pallas_call(
        moe_kernel,
        out_shape=tuple(vmem(r.shape, r.dtype) for r in results),
        in_specs=[anywhere] * 5,
        out_specs=(pl.BlockSpec(memory_space=pltpu.VMEM),) * 4,
        scratch_shapes=[
            vmem((TOK, D), BF16),
            vmem((TOPK, TOK), jnp.int32),
            vmem((TOPK, TOK), F32),
            vmem((TOK, D), BF16),
        ]
        + [
            vmem((3, 2, NZ, CHUNK, FF), BF16),
            vmem((HELD, TOK), F32),
            vmem((HELD, TOK), F32),
            vmem((PACK, 2 * TOK), F32),
            vmem((PACK, 2 * TOK), BF16),
            vmem((PACK, 2 * TOK), F32),
        ]
        + [vmem((2 * TOK, PACK), BF16)] * 3
        + [vmem((PACK, TOK), F32)]
        + [vmem((PACK, HALF), BF16)] * 6
        + [
            vmem((2, ROWS, HALF), BF16),
            vmem((2, 2 * ROWS, HALF), BF16),
            vmem((HALF, 2 * ROWS), BF16),
            vmem((HALF, ROWS), BF16),
            vmem((ROWS, FF), BF16),
            vmem((FF, 2 * ROWS), BF16),
            vmem((ROWS, FF), F32),
            vmem((ROWS, FF), F32),
            vmem((2, 2 * ROWS, FF), BF16),
            vmem((2, HALF, FF), F32),
            vmem((FF, HALF), F32),
        ]
        + [vmem(((NZ - 1) * 4, PIECE, FF), BF16)] * 2
        + [vmem(((NZ - 1) * 2, HIDDEN_PIECE, CHUNK), BF16)] * 2
        + [dma((4,)), dma((6,))]
        + [dma((HELD,))] * 8
        + [dma((2 + HELD // 2 + 6,))] * 2
        + [dma(((NZ - 1) * 6,))] * 2,
        compiler_params=pltpu.CompilerParams(
            collective_id=0, has_side_effects=True, vmem_limit_bytes=60 << 20
        ),
    )(tokens, expert_ids.T, gate_probs.T, cotangent, weights)
    made = [pltpu.with_memory_space_constraint(m, pltpu.VMEM) for m in made]
    mixed, grad_tok, grad_gate, grad_w = pl.pallas_call(
        hand_out,
        out_shape=results,
        in_specs=[pl.BlockSpec(memory_space=pltpu.VMEM)] * 4,
        out_specs=(anywhere,) * 4,
        scratch_shapes=[dma((4,))],
    )(*made)
    return mixed, grad_tok, grad_gate.T, jnp.transpose(grad_w, (1, 0, 2))[:, None]


def solution(mesh):
    rows = P(("dp", "expert"), None)
    return jax.shard_map(
        per_device,
        mesh=mesh,
        in_specs=(rows, rows, rows, rows, P(None, "expert", None, None)),
        out_specs=(rows, rows, rows, P("dp", "expert", None, None)),
        check_vma=False,
    )
```

time: 118 us -> 104 us (0.88)
  the two profiles are of different devices: /device:TPU:28 before, /device:TPU:8 now
where the time goes in v2:
time: 104 us
  Pallas kernels  103 us (99%)
    pallas_call x1, Pallas kernels, per_device(): pl.pallas_call(moe_kernel, out_shape=tuple((vmem(r.shape, r.dtype) for r...  102 us

profile of v2, /device:TPU:8, one launch (start us, length us, event | category | flops | bytes accessed | tf_op | source)
XLA Modules:
  0.0 104.1 jit_solution(14928415779610720575)
XLA Ops:
  0.6 102.3 %shard_map.84 = (bf16[128,2048]{1,0:T(8,128)(2,1)S(1)}, bf16[128,2048]{1,0:T(8,128)(2,1)S(1)}, f32[8,128]{1,0:T(8,128)S(1)}, bf16[3,128,768]{2,1,0:T(8,128)(2,1)S(1)}) custom-call(bf16[128,2048]{1,0:T(8,128)(2,1)} %tok_hbm.1, s32[8,128]{1,0:T(8,128)} %bitcast.12, f32[8,128]{1,0:T(8,128)} %bitcast.13, bf16[128,2048]{1,0:T(8,128)(2,1)} %cot_hbm.1, ...), custom_call_target="tpu_custom_call" | custom-call | tf_op jit(solution)/shard_map/pallas_call | solution.py:442
  102.9 1.2 %shard_map.85 = (bf16[128,2048]{1,0:T(8,128)(2,1)}, bf16[128,2048]{1,0:T(8,128)(2,1)}, f32[8,128]{1,0:T(8,128)}, bf16[3,128,768]{2,1,0:T(8,128)(2,1)}) custom-call(bf16[128,2048]{1,0:T(8,128)(2,1)S(1)} %get-tuple-element.12.refs_0_, bf16[128,2048]{1,0:T(8,128)(2,1)S(1)} %get-tuple-element.13.refs_1_, f32[8,128]{1,0:T(8,128)S(1)} %get-tuple-element.14.refs_2_, ...), custom_call_target="tpu_custom_call" | custom-call | tf_op jit(solution)/shard_map/pallas_call | solution.py:488

commit v3 on v2

--- a/solution.py
+++ b/solution.py
@@ -21,10 +21,10 @@
 CHUNK = D // (2 * NZ)
 PIECE = CHUNK // 2
 HIDDEN_PIECE = FF // 2
-ORDER = (2, 0, 1)
+PART = HALF // 2
 OFFSETS = (
-    (0, 0), (0, 1), (1, 0), (0, 3), (3, 0), (0, 2), (2, 0), (1, 1),
-    (3, 3), (1, 3), (3, 1), (2, 1), (1, 2), (2, 3), (3, 2), (2, 2),
+    (0, 0), (2, 2), (0, 2), (2, 0), (1, 2), (2, 1), (3, 2), (2, 3),
+    (1, 1), (3, 3), (1, 3), (3, 1), (0, 1), (1, 0), (0, 3), (3, 0),
 )
 BF16 = jnp.bfloat16
 F32 = jnp.float32
@@ -44,10 +44,10 @@
     mixed, grad_tok, grad_gate, grad_w,
     tok, ids, probs, cot,
     w, place, held_prob, onehot, onehot_b, prob, onehot_t, prob_hi, prob_lo, gate_acc,
-    send_x, send_dy, recv_x, recv_dy, recv_out, recv_part,
-    xs, dys, x_mine, x_other, hidden, hidden_t, acts, silus, rights, grads, grads_t,
+    send_x, send_dy, send_part, recv_x, recv_dy, recv_out, recv_part,
+    xs, dys, x_mine, x_other, hidden, hidden_t, acts, silus, partial, rights, grads, grads_t,
     ring_send, ring_recv, ring_send_t, ring_recv_t,
-    in_sem, w_sem, x_ss, x_rs, dy_ss, dy_rs, out_ss, out_rs, part_ss, part_rs,
+    in_sem, w_sem, x_ss, x_rs, dy_ss, dy_rs, late_ss, late_rs, out_ss, out_rs, part_ss, part_rs,
     sib_ss, sib_rs, ring_ss, ring_rs,
 ):
     dp, ex = lax.axis_index("dp"), lax.axis_index("expert")
@@ -72,10 +72,23 @@
     ]
     for c in loads:
         c.start()
+    def near_chunk(j, c):
+        if c == 0:
+            return lax.rem(z + NZ - 1 - j, NZ)
+        return lax.rem(z + 1 + j + NZ // 2 * (j // (TILES - 1)), NZ)
+
     w_copies = [
-        pltpu.make_async_copy(w_hbm.at[m, :, par], w.at[m, par], w_sem.at[2 * m + par])
-        for m in range(3)
-        for par in range(2)
+        pltpu.make_async_copy(w_hbm.at[m, :, h], w.at[m, h], w_sem.at[2 * m + h])
+        for m in range(2)
+        for h in range(2)
+    ]
+    w_copies += [
+        pltpu.make_async_copy(
+            w_hbm.at[2, near_chunk(j, c), h], w.at[2, h, 2 * j + c], w_sem.at[4 + (2 * j + c) * 2 + h]
+        )
+        for j in range(TILES)
+        for c in range(2)
+        for h in range(2)
     ]
 
     barrier = pltpu.get_barrier_semaphore()
@@ -116,10 +129,12 @@
     def chunk_columns(j, c, h):
         return pl.ds(pl.multiple_of((4 * j + 2 * c + h) * CHUNK, CHUNK), CHUNK)
 
-    def stacked(ref, j):
+    def near_columns(j, c, h):
+        return pl.ds(pl.multiple_of((2 * near_chunk(j, c) + h) * CHUNK, CHUNK), CHUNK)
+
+    def stacked(ref, j, at):
         halves = [
-            jnp.concatenate([ref[:, chunk_columns(j, c, h)] for c in range(2)], axis=1)
-            for h in range(2)
+            jnp.concatenate([ref[:, at(j, c, h)] for c in range(2)], axis=1) for h in range(2)
         ]
         return jnp.concatenate(halves, axis=0)
 
@@ -153,9 +168,12 @@
         pltpu.make_async_copy(dst.at[rows], dst.at[rows], recv_sem.at[n]).wait()
 
     x_way = (send_x, recv_x, x_ss, x_rs)
-    dy_way = (send_dy, recv_dy, dy_ss, dy_rs)
+    dy_ways = (
+        (send_dy.at[0], recv_dy.at[0], dy_ss, dy_rs),
+        (send_dy.at[1], recv_dy.at[1], late_ss, late_rs),
+    )
     out_way = (send_x, recv_out, out_ss, out_rs)
-    part_way = (send_dy, recv_part, part_ss, part_rs)
+    part_way = (send_part, recv_part, part_ss, part_rs)
     everyone = range(HELD)
 
     for group in range(2):
@@ -170,7 +188,7 @@
                 c.start()
 
         def pack_x(j, _, rows=rows):
-            send_x[rows, columns(j)] = dot(onehot_b[rows, :], stacked(tok, j)).astype(BF16)
+            send_x[rows, columns(j)] = dot(onehot_b[rows, :], stacked(tok, j, chunk_columns)).astype(BF16)
             return 0
 
         lax.fori_loop(0, TILES, pack_x, 0)
@@ -183,13 +201,11 @@
     row_prob = jnp.sum(prob[...], axis=1, keepdims=True)
     loads[3].wait()
 
-    def pack_dy(j, _):
-        picked = dot(onehot_b[...], stacked(cot, j))
-        send_dy[:, columns(j)] = (row_prob * picked).astype(BF16)
-        return 0
-
-    lax.fori_loop(0, TILES, pack_dy, 0)
-    send_blocks(everyone, 1, *dy_way)
+    for part in range(2):
+        for j in range(TILES // 2):
+            picked = dot(onehot_b[...], stacked(cot, part * TILES // 2 + j, near_columns))
+            send_dy[part, :, columns(j)] = (row_prob * picked).astype(BF16)
+        send_blocks(everyone, 1, *dy_ways[part])
 
     onehot_t[...] = jnp.transpose(onehot[...]).astype(BF16)
     prob_t = jnp.transpose(prob[...])
@@ -207,16 +223,18 @@
     x_over = to_sibling(0, x_other, x_mine.at[:, theirs])
     hidden_over = to_sibling(1, hidden_t.at[:, own], hidden_t.at[:, theirs])
 
-    def dy_over(i):
+    def dy_over(part, i):
         rows = pl.ds(pl.multiple_of(i * BLK, BLK), BLK)
         there = pl.ds(pl.multiple_of(ROWS + i * BLK, BLK), BLK)
-        return to_sibling(2 + i, dys.at[1 - core, rows], dys.at[1 - core, there])
+        cols = pl.ds(PART * part, PART)
+        src, dst = dys.at[1 - core, rows, cols], dys.at[1 - core, there, cols]
+        return to_sibling(2 + HELD // 2 * part + i, src, dst)
 
     def grad_over(m, j):
         src, dst = rights.at[m, own, columns(j)], rights.at[m, theirs, columns(j)]
-        return to_sibling(2 + HELD // 2 + 3 * m + j, src, dst)
-
-    def unpack(recv, recv_sem, full, then=None):
+        return to_sibling(2 + HELD + 3 * m + j, src, dst)
+
+    def unpack(recv, recv_sem, full, cols, then=None):
         def one(i, _):
             wait_block(2 * i, recv, recv_sem)
             wait_block(2 * i + 1, recv, recv_sem)
@@ -224,7 +242,7 @@
             rows = pl.ds(pl.multiple_of(i * BLK, BLK), BLK)
             for h in range(2):
                 parts = [v[CAP * (2 * b + h) : CAP * (2 * b + h + 1)] for b in range(2)]
-                full[h, rows, :] = jnp.concatenate(parts, axis=0).astype(BF16)
+                full[h, rows, cols] = jnp.concatenate(parts, axis=0).astype(BF16)
             if then is not None:
                 then(i).start()
             return 0
@@ -234,7 +252,7 @@
     def weight(m, h, j):
         return w[m, h, :, :, columns(j)].reshape(HALF, TILE)
 
-    unpack(recv_x, x_rs, xs)
+    unpack(recv_x, x_rs, xs, pl.ds(0, HALF))
     for c in w_copies:
         c.wait()
 
@@ -277,21 +295,19 @@
         repack(send_x, j, left, right)
         return 0
 
-    lax.fori_loop(0, TILES, expert_out, 0)
-    unpack(recv_dy, dy_rs, dys, dy_over)
-    send_blocks(everyone, -1, *out_way)
-
-    for j in range(FF // TILE):
-        hg = dot(dys[0, own, :], weight(2, 0, j)) + dot(dys[1, own, :], weight(2, 1, j))
-        rights[0, own, columns(j)] = (hg * acts[:, columns(j)]).astype(BF16)
-        rights[1, own, columns(j)] = (hg * silus[:, columns(j)]).astype(BF16)
-        grad_over(0, j).start()
-        grad_over(1, j).start()
-
-    def piece(m, way, chunk):
+    def piece(m, way, distance):
         if m == 2:
-            cols = pl.ds(pl.multiple_of(chunk * CHUNK, CHUNK), CHUNK)
+            if distance == NZ:
+                place_at = NZ - 1
+            elif distance < NZ // 2 or (distance == NZ // 2 and way == 0):
+                place_at = 2 * (distance - 1) + way
+            elif distance == NZ // 2:
+                place_at = NZ - 2
+            else:
+                place_at = 2 * (NZ - 1 - distance) + 1 - way
+            cols = pl.ds(CHUNK * place_at, CHUNK)
             return grads_t[HIDDEN_PIECE * way : HIDDEN_PIECE * (way + 1), cols]
+        chunk = lax.rem(z + (NZ - distance if way == 0 else distance), NZ)
         return grads[m, pl.ds(pl.multiple_of(chunk * CHUNK + way * PIECE, PIECE), PIECE), :]
 
     def slots(m, way, step):
@@ -310,80 +326,129 @@
             device_id=(after, before)[way],
         )
 
-    def chunk_at(way, distance):
-        return lax.rem(z + (NZ - distance if way == 0 else distance), NZ)
-
     def begin(m):
         for way in range(2):
             src, _, n = slots(m, way, 0)
-            src[n] = piece(m, way, chunk_at(way, 1)).astype(BF16)
+            src[n] = piece(m, way, 1).astype(BF16)
             ring(m, way, 0).start()
 
-    hidden_over.wait()
-    for i in range(HELD // 2):
-        dy_over(i).wait()
-
-    def down_grad(j, _):
-        grads_t[:, columns(j)] = dot(hidden_t[...], dys[core, :, columns(j)])
-        return 0
-
-    lax.fori_loop(0, TILES, down_grad, 0)
-    begin(2)
-    x_over.wait()
-    for m in range(2):
-        for j in range(FF // TILE):
-            grad_over(m, j).wait()
-
-        def weight_grad(j, _, m=m):
-            grads[m, :, columns(j)] = dot(x_mine[...], rights[m, :, columns(j)])
-            return 0
-
-        lax.fori_loop(0, FF // TILE, weight_grad, 0)
-        begin(m)
-
-    wait_sent(1, *dy_way)
-
-    def token_part(j, _):
+    def pass_on(m, step):
+        for way in range(2):
+            ring(m, way, step).wait_recv()
+            src, dst, n = slots(m, way, step)
+            total = dst[n].astype(F32) + piece(m, way, step + 2)
+            src[n + (2 if m == 2 else 4)] = total.astype(BF16)
+            ring(m, way, step + 1).start()
+
+    def finish(m):
+        for way in range(2):
+            ring(m, way, NZ - 2).wait_recv()
+            _, dst, n = slots(m, way, NZ - 2)
+            total = dst[n].astype(F32) + piece(m, way, NZ)
+            if m == 2:
+                cols = pl.ds(HIDDEN_PIECE * way, HIDDEN_PIECE)
+                grad_w[m, :, cols] = jnp.transpose(total).astype(BF16)
+            else:
+                grad_w[m, PIECE * way : PIECE * (way + 1), :] = total.astype(BF16)
+
+    def down_grad(part):
+        for i in range(HELD // 2):
+            dy_over(part, i).wait()
+        for j in range(TILES // 2 * part, TILES // 2 * (part + 1)):
+            grads_t[:, columns(j)] = dot(hidden_t[...], dys[core, :, columns(j)])
+
+    def half_hidden_grad(part, j):
+        cols = pl.ds(PART * part, PART)
+        near = pl.ds(NZ // 2 * part, NZ // 2)
+        terms = [
+            dot(dys[h, own, cols], w[2, h, near, :, columns(j)].reshape(PART, TILE)) for h in range(2)
+        ]
+        return terms[0] + terms[1]
+
+    def token_part(j):
         gate_g, up_g = rights[0, own, :], rights[1, own, :]
         left, right = [
             dot_nt(gate_g, weight_rows(0, h, j)) + dot_nt(up_g, weight_rows(1, h, j))
             for h in range(2)
         ]
-        repack(send_dy, j, left, right)
-        return 0
-
-    lax.fori_loop(0, TILES, token_part, 0)
+        repack(send_part, j, left, right)
+
+    def weight_grad(m):
+        for j in range(FF // TILE):
+            grad_over(m, j).wait()
+
+        def one(j, _):
+            grads[m, :, columns(j)] = dot(x_mine[...], rights[m, :, columns(j)])
+            return 0
+
+        lax.fori_loop(0, FF // TILE, one, 0)
+
+    unpack(*dy_ways[0][1::2], dys, pl.ds(0, PART), lambda i: dy_over(0, i))
+    hidden_over.wait()
+    down_grad(0)
+    begin(2)
+
+    def first_half(j, _):
+        partial[:, columns(j)] = half_hidden_grad(0, j)
+        return 0
+
+    lax.fori_loop(0, FF // TILE, first_half, 0)
+    lax.fori_loop(0, TILES, expert_out, 0)
+    pass_on(2, 0)
+    unpack(*dy_ways[1][1::2], dys, pl.ds(PART, PART), lambda i: dy_over(1, i))
+    send_blocks(everyone, -1, *out_way)
+    for j in range(FF // TILE):
+        hg = partial[:, columns(j)] + half_hidden_grad(1, j)
+        rights[0, own, columns(j)] = (hg * acts[:, columns(j)]).astype(BF16)
+        rights[1, own, columns(j)] = (hg * silus[:, columns(j)]).astype(BF16)
+        grad_over(0, j).start()
+        grad_over(1, j).start()
+    down_grad(1)
+    pass_on(2, 1)
+    x_over.wait()
+    weight_grad(0)
+    begin(0)
+    pass_on(2, 2)
+    weight_grad(1)
+    begin(1)
+    token_part(0)
+    token_part(1)
+    pass_on(0, 0)
+    token_part(2)
+    token_part(3)
+    pass_on(2, 3)
+    pass_on(1, 0)
     send_blocks(everyone, -1, *part_way)
-
-    def pass_on(step, _):
-        for m in ORDER:
-            for way in range(2):
-                ring(m, way, step).wait_recv()
-                src, dst, n = slots(m, way, step)
-                total = dst[n].astype(F32) + piece(m, way, chunk_at(way, step + 2))
-                src[n + (2 if m == 2 else 4)] = total.astype(BF16)
-                ring(m, way, step + 1).start()
-        return 0
-
-    lax.fori_loop(0, NZ - 2, pass_on, 0)
+    for step in range(1, 3):
+        pass_on(0, step)
+        pass_on(2, step + 3)
+        pass_on(1, step)
+
+    def last_steps(step, _):
+        pass_on(0, step)
+        pass_on(1, step)
+        return 0
+
+    lax.fori_loop(3, NZ - 2, last_steps, 0)
+    finish(2)
 
     for n in everyone:
         wait_block(n, recv_out, out_rs)
         wait_block(n, recv_part, part_rs)
     gate_acc[...] = jnp.zeros_like(gate_acc)
 
-    def spread(ref, j, value):
+    def spread(ref, j, at, value):
         for h in range(2):
             for c in range(2):
-                ref[:, chunk_columns(j, c, h)] = value[
+                ref[:, at(j, c, h)] = value[
                     TOK * h : TOK * (h + 1), CHUNK * c : CHUNK * (c + 1)
                 ].astype(BF16)
 
     def combine(j, _):
         back = recv_out[:, columns(j)]
-        spread(mixed, j, dot(prob_hi[...], back) + dot(prob_lo[...], back))
-        spread(grad_tok, j, dot(onehot_t[...], recv_part[:, columns(j)]))
-        product = back.astype(F32) * dot(onehot_b[...], stacked(cot, j))
+        spread(mixed, j, near_columns, dot(prob_hi[...], back) + dot(prob_lo[...], back))
+        spread(grad_tok, j, chunk_columns, dot(onehot_t[...], recv_part[:, columns(j)]))
+        product = back.astype(F32) * dot(onehot_b[...], stacked(cot, j, near_columns))
         gate_acc[...] += product[:, 0:TOK] + product[:, TOK : 2 * TOK]
         return 0
 
@@ -396,22 +461,15 @@
         result = jnp.where(ids[...] == peer(n), value, result)
     grad_gate[...] = result
 
-    for m in ORDER:
-        for way in range(2):
-            ring(m, way, NZ - 2).wait_recv()
-            _, dst, n = slots(m, way, NZ - 2)
-            total = dst[n].astype(F32) + piece(m, way, z)
-            if m == 2:
-                cols = pl.ds(HIDDEN_PIECE * way, HIDDEN_PIECE)
-                grad_w[m, :, cols] = jnp.transpose(total).astype(BF16)
-            else:
-                grad_w[m, PIECE * way : PIECE * (way + 1), :] = total.astype(BF16)
-
+    finish(0)
+    finish(1)
+    for way in dy_ways:
+        wait_sent(1, *way)
     wait_sent(-1, *out_way)
     wait_sent(-1, *part_way)
 
     def wait_ring(step, _):
-        for m in ORDER:
+        for m in range(3):
             for way in range(2):
                 ring(m, way, step).wait_send()
         return 0
@@ -460,7 +518,9 @@
         ]
         + [vmem((2 * TOK, PACK), BF16)] * 3
         + [vmem((PACK, TOK), F32)]
-        + [vmem((PACK, HALF), BF16)] * 6
+        + [vmem((PACK, HALF), BF16), vmem((2, PACK, PART), BF16), vmem((PACK, HALF), BF16)]
+        + [vmem((PACK, HALF), BF16), vmem((2, PACK, PART), BF16)]
+        + [vmem((PACK, HALF), BF16)] * 2
         + [
             vmem((2, ROWS, HALF), BF16),
             vmem((2, 2 * ROWS, HALF), BF16),
@@ -470,15 +530,16 @@
             vmem((FF, 2 * ROWS), BF16),
             vmem((ROWS, FF), F32),
             vmem((ROWS, FF), F32),
+            vmem((ROWS, FF), F32),
             vmem((2, 2 * ROWS, FF), BF16),
             vmem((2, HALF, FF), F32),
             vmem((FF, HALF), F32),
         ]
         + [vmem(((NZ - 1) * 4, PIECE, FF), BF16)] * 2
         + [vmem(((NZ - 1) * 2, HIDDEN_PIECE, CHUNK), BF16)] * 2
-        + [dma((4,)), dma((6,))]
-        + [dma((HELD,))] * 8
-        + [dma((2 + HELD // 2 + 6,))] * 2
+        + [dma((4,)), dma((4 + 2 * NZ,))]
+        + [dma((HELD,))] * 10
+        + [dma((2 + HELD + 6,))] * 2
         + [dma(((NZ - 1) * 6,))] * 2,
         compiler_params=pltpu.CompilerParams(
             collective_id=0, has_side_effects=True, vmem_limit_bytes=60 << 20

time: 104 us -> 99.5 us (0.957)
  the two profiles are of different devices: /device:TPU:8 before, /device:TPU:18 now
where the time goes in v3:
time: 99.5 us; the launch traced here: 99.3 us
  Pallas kernels  98.7 us (99%)
    pallas_call x1, Pallas kernels, per_device(): pl.pallas_call(moe_kernel, out_shape=tuple((vmem(r.shape, r.dtype) for r...  97.5 us

profile of v3, /device:TPU:18, one launch (start us, length us, event | category | flops | bytes accessed | tf_op | source)
XLA Modules:
  0.0 99.3 jit_solution(4575912146812633542)
XLA Ops:
  0.6 97.5 %shard_map.84 = (bf16[128,2048]{1,0:T(8,128)(2,1)S(1)}, bf16[128,2048]{1,0:T(8,128)(2,1)S(1)}, f32[8,128]{1,0:T(8,128)S(1)}, bf16[3,128,768]{2,1,0:T(8,128)(2,1)S(1)}) custom-call(bf16[128,2048]{1,0:T(8,128)(2,1)} %tok_hbm.1, s32[8,128]{1,0:T(8,128)} %bitcast.12, f32[8,128]{1,0:T(8,128)} %bitcast.13, bf16[128,2048]{1,0:T(8,128)(2,1)} %cot_hbm.1, ...), custom_call_target="tpu_custom_call" | custom-call | tf_op jit(solution)/shard_map/pallas_call | solution.py:500
  98.1 1.2 %shard_map.85 = (bf16[128,2048]{1,0:T(8,128)(2,1)}, bf16[128,2048]{1,0:T(8,128)(2,1)}, f32[8,128]{1,0:T(8,128)}, bf16[3,128,768]{2,1,0:T(8,128)(2,1)}) custom-call(bf16[128,2048]{1,0:T(8,128)(2,1)S(1)} %get-tuple-element.12.refs_0_, bf16[128,2048]{1,0:T(8,128)(2,1)S(1)} %get-tuple-element.13.refs_1_, f32[8,128]{1,0:T(8,128)S(1)} %get-tuple-element.14.refs_2_, ...), custom_call_target="tpu_custom_call" | custom-call | tf_op jit(solution)/shard_map/pallas_call | solution.py:549

commit v4 on v3

--- a/solution.py
+++ b/solution.py
@@ -19,8 +19,9 @@
 TILE = 256
 TILES = HALF // TILE
 CHUNK = D // (2 * NZ)
-PIECE = CHUNK // 2
-HIDDEN_PIECE = FF // 2
+SUBS = 2
+PIECE = CHUNK // 2 // SUBS
+HIDDEN_PIECE = FF // 2 // SUBS
 PART = HALF // 2
 OFFSETS = (
     (0, 0), (2, 2), (0, 2), (2, 0), (1, 2), (2, 1), (3, 2), (2, 3),
@@ -46,7 +47,7 @@
     w, place, held_prob, onehot, onehot_b, prob, onehot_t, prob_hi, prob_lo, gate_acc,
     send_x, send_dy, send_part, recv_x, recv_dy, recv_out, recv_part,
     xs, dys, x_mine, x_other, hidden, hidden_t, acts, silus, partial, rights, grads, grads_t,
-    ring_send, ring_recv, ring_send_t, ring_recv_t,
+    ring_send, ring_recv, ring_send_t, ring_recv_t, hidden_flip,
     in_sem, w_sem, x_ss, x_rs, dy_ss, dy_rs, late_ss, late_rs, out_ss, out_rs, part_ss, part_rs,
     sib_ss, sib_rs, ring_ss, ring_rs,
 ):
@@ -295,7 +296,7 @@
         repack(send_x, j, left, right)
         return 0
 
-    def piece(m, way, distance):
+    def piece(m, way, sub, distance):
         if m == 2:
             if distance == NZ:
                 place_at = NZ - 1
@@ -306,18 +307,19 @@
             else:
                 place_at = 2 * (NZ - 1 - distance) + 1 - way
             cols = pl.ds(CHUNK * place_at, CHUNK)
-            return grads_t[HIDDEN_PIECE * way : HIDDEN_PIECE * (way + 1), cols]
+            return grads_t[pl.ds(HIDDEN_PIECE * (SUBS * way + sub), HIDDEN_PIECE), cols]
         chunk = lax.rem(z + (NZ - distance if way == 0 else distance), NZ)
-        return grads[m, pl.ds(pl.multiple_of(chunk * CHUNK + way * PIECE, PIECE), PIECE), :]
-
-    def slots(m, way, step):
+        first = chunk * CHUNK + (SUBS * way + sub) * PIECE
+        return grads[m, pl.ds(pl.multiple_of(first, PIECE), PIECE), :]
+
+    def slots(m, way, sub, step):
         if m == 2:
-            return ring_send_t, ring_recv_t, step * 2 + way
-        return ring_send, ring_recv, (step * 2 + m) * 2 + way
-
-    def ring(m, way, step):
-        src, dst, n = slots(m, way, step)
-        k = (step * 3 + m) * 2 + way
+            return ring_send_t, ring_recv_t, (step * 2 + way) * SUBS + sub
+        return ring_send, ring_recv, ((step * 2 + m) * 2 + way) * SUBS + sub
+
+    def ring(m, way, sub, step):
+        src, dst, n = slots(m, way, sub, step)
+        k = ((step * 3 + m) * 2 + way) * SUBS + sub
         return pltpu.make_async_remote_copy(
             src_ref=src.at[n],
             dst_ref=dst.at[n],
@@ -326,30 +328,34 @@
             device_id=(after, before)[way],
         )
 
+    both_ways = [(way, sub) for sub in range(SUBS) for way in range(2)]
+
     def begin(m):
-        for way in range(2):
-            src, _, n = slots(m, way, 0)
-            src[n] = piece(m, way, 1).astype(BF16)
-            ring(m, way, 0).start()
+        for way, sub in both_ways:
+            src, _, n = slots(m, way, sub, 0)
+            src[n] = piece(m, way, sub, 1).astype(BF16)
+            ring(m, way, sub, 0).start()
 
     def pass_on(m, step):
-        for way in range(2):
-            ring(m, way, step).wait_recv()
-            src, dst, n = slots(m, way, step)
-            total = dst[n].astype(F32) + piece(m, way, step + 2)
-            src[n + (2 if m == 2 else 4)] = total.astype(BF16)
-            ring(m, way, step + 1).start()
+        for way, sub in both_ways:
+            ring(m, way, sub, step).wait_recv()
+            src, dst, n = slots(m, way, sub, step)
+            total = dst[n].astype(F32) + piece(m, way, sub, step + 2)
+            src[n + (2 if m == 2 else 4) * SUBS] = total.astype(BF16)
+            ring(m, way, sub, step + 1).start()
 
     def finish(m):
-        for way in range(2):
-            ring(m, way, NZ - 2).wait_recv()
-            _, dst, n = slots(m, way, NZ - 2)
-            total = dst[n].astype(F32) + piece(m, way, NZ)
+        for way, sub in both_ways:
+            ring(m, way, sub, NZ - 2).wait_recv()
+            _, dst, n = slots(m, way, sub, NZ - 2)
+            total = dst[n].astype(F32) + piece(m, way, sub, NZ)
+            k = SUBS * way + sub
             if m == 2:
-                cols = pl.ds(HIDDEN_PIECE * way, HIDDEN_PIECE)
-                grad_w[m, :, cols] = jnp.transpose(total).astype(BF16)
+                hidden_flip[pl.ds(HIDDEN_PIECE * k, HIDDEN_PIECE), :] = total
             else:
-                grad_w[m, PIECE * way : PIECE * (way + 1), :] = total.astype(BF16)
+                grad_w[m, pl.ds(PIECE * k, PIECE), :] = total.astype(BF16)
+        if m == 2:
+            grad_w[m] = jnp.transpose(hidden_flip[...]).astype(BF16)
 
     def down_grad(part):
         for i in range(HELD // 2):
@@ -412,12 +418,12 @@
     weight_grad(1)
     begin(1)
     token_part(0)
+    pass_on(0, 0)
     token_part(1)
-    pass_on(0, 0)
+    pass_on(2, 3)
     token_part(2)
+    pass_on(1, 0)
     token_part(3)
-    pass_on(2, 3)
-    pass_on(1, 0)
     send_blocks(everyone, -1, *part_way)
     for step in range(1, 3):
         pass_on(0, step)
@@ -470,8 +476,8 @@
 
     def wait_ring(step, _):
         for m in range(3):
-            for way in range(2):
-                ring(m, way, step).wait_send()
+            for way, sub in both_ways:
+                ring(m, way, sub, step).wait_send()
         return 0
 
     lax.fori_loop(0, NZ - 1, wait_ring, 0)
@@ -535,12 +541,13 @@
             vmem((2, HALF, FF), F32),
             vmem((FF, HALF), F32),
         ]
-        + [vmem(((NZ - 1) * 4, PIECE, FF), BF16)] * 2
-        + [vmem(((NZ - 1) * 2, HIDDEN_PIECE, CHUNK), BF16)] * 2
+        + [vmem(((NZ - 1) * 4 * SUBS, PIECE, FF), BF16)] * 2
+        + [vmem(((NZ - 1) * 2 * SUBS, HIDDEN_PIECE, CHUNK), BF16)] * 2
+        + [vmem((FF, CHUNK), F32)]
         + [dma((4,)), dma((4 + 2 * NZ,))]
         + [dma((HELD,))] * 10
         + [dma((2 + HELD + 6,))] * 2
-        + [dma(((NZ - 1) * 6,))] * 2,
+        + [dma(((NZ - 1) * 6 * SUBS,))] * 2,
         compiler_params=pltpu.CompilerParams(
             collective_id=0, has_side_effects=True, vmem_limit_bytes=60 << 20
         ),

time: 99.5 us -> 99.6 us (level)
  no operation moved by 1% of the time
where the time goes in v4:
time: 99.6 us; the launch traced here: 99.4 us
  Pallas kernels  98.8 us (99%)
    pallas_call x1, Pallas kernels, per_device(): pl.pallas_call(moe_kernel, out_shape=tuple((vmem(r.shape, r.dtype) for r...  97.6 us

profile of v4, /device:TPU:18, one launch (start us, length us, event | category | flops | bytes accessed | tf_op | source)
XLA Modules:
  0.0 99.4 jit_solution(14259131672334975723)
XLA Ops:
  0.6 97.6 %shard_map.84 = (bf16[128,2048]{1,0:T(8,128)(2,1)S(1)}, bf16[128,2048]{1,0:T(8,128)(2,1)S(1)}, f32[8,128]{1,0:T(8,128)S(1)}, bf16[3,128,768]{2,1,0:T(8,128)(2,1)S(1)}) custom-call(bf16[128,2048]{1,0:T(8,128)(2,1)} %tok_hbm.1, s32[8,128]{1,0:T(8,128)} %bitcast.12, f32[8,128]{1,0:T(8,128)} %bitcast.13, bf16[128,2048]{1,0:T(8,128)(2,1)} %cot_hbm.1, ...), custom_call_target="tpu_custom_call" | custom-call | tf_op jit(solution)/shard_map/pallas_call | solution.py:506
  98.2 1.2 %shard_map.85 = (bf16[128,2048]{1,0:T(8,128)(2,1)}, bf16[128,2048]{1,0:T(8,128)(2,1)}, f32[8,128]{1,0:T(8,128)}, bf16[3,128,768]{2,1,0:T(8,128)(2,1)}) custom-call(bf16[128,2048]{1,0:T(8,128)(2,1)S(1)} %get-tuple-element.12.refs_0_, bf16[128,2048]{1,0:T(8,128)(2,1)S(1)} %get-tuple-element.13.refs_1_, f32[8,128]{1,0:T(8,128)S(1)} %get-tuple-element.14.refs_2_, ...), custom_call_target="tpu_custom_call" | custom-call | tf_op jit(solution)/shard_map/pallas_call | solution.py:556
